TPU v7x, 32 devices: a whole 2x2x4 slice. The times are simulated.
32 devices in a mesh: section: 4 (over y, core), dp: 4 (over z), tensor: 2 (over x).
Axes of the slice: x: 2, y: 2, z: 4, core: 2. Of those that a mesh axis runs over, the one named last changes fastest.
Arguments:
- out_grad: bfloat16 [512, 4096], P('dp', 'tensor'), may hold values from -6 to 6
- section_out: bfloat16 [4, 512, 4096], P('section', 'dp', 'tensor'), may hold values from -6 to 6
- context: bfloat16 [4, 512, 2048], P('section', 'dp', 'tensor'), may hold values from -6 to 6
- queries: bfloat16 [4, 512, 2048], P('section', 'dp', 'tensor')
- key_heads: bfloat16 [4, 512, 2048], P('section', 'dp', 'tensor')
- values: bfloat16 [4, 512, 2048], P('section', 'dp', 'tensor'), may hold values from -6 to 6
- o_weight: bfloat16 [4, 4096, 2048], P('section', None, 'tensor'), may hold values from -0.125 to 0.125
- doc_lengths: int32 [4], replicated, may hold values from 1 to 256, 512 in all
Outputs:
- query_grad: bfloat16 [4, 512, 2048], P('section', 'dp', 'tensor')
- key_grad: bfloat16 [4, 512, 2048], P('section', 'dp', 'tensor')
- value_grad: bfloat16 [4, 512, 2048], P('section', 'dp', 'tensor')
- o_weight_grad: float32 [4, 4096, 2048], P('section', 'dp', 'tensor')
Inputs may be any that keep to these rules, and one draw needn't show every extreme that they name: `doc_lengths`: the lengths sum to 512, and the longest document has exactly 256 patches.
All inputs are finite; a program needn't handle non-finite values.
Results may differ from a plain program's by a relative error of at most 0.023.
Values may be sent and summed in bfloat16 or wider, within the bound.
A program may use at most 64 MiB of HBM per device.

v0:
```python
import jax
import jax.numpy as jnp
from jax import lax
from jax.sharding import PartitionSpec as P

HD = 128
REACH = 2


def entering(value, axis, combine, identity):
    count, position = (lax.axis_size(axis), lax.axis_index(axis))
    everything = lax.all_gather(value.astype(jnp.bfloat16), axis)
    start = jnp.broadcast_to(jnp.asarray(identity, value.dtype), value.shape)

    def hop(k, before):
        at = count - 1 - k
        reached = at > position
        new = combine(before, everything[at].astype(value.dtype))
        return jnp.where(reached, new, before)

    return lax.fori_loop(0, count, hop, start)


def passed_along(value, axis, steps):
    count = lax.axis_size(axis)
    leading, last = (max(0, -steps), min(count, count - steps))
    return lax.ppermute(value, axis, [(source, source + steps) for source in range(leading, last)])


def add_pair(earlier, later):
    return earlier + later


def document_of(positions, ends):
    return jnp.sum((positions[:, None] >= ends[None, :]).astype(jnp.int32), axis=-1)


def on_device(out_grad, section_out, context, queries, key_heads, values, o_weight, doc_lengths):
    rows, width = (queries.shape[1], queries.shape[2])
    head_count = width // HD
    scaling = HD ** (-0.5)
    own_out = section_out[0].astype(jnp.float32)
    above = entering(own_out, "section", add_pair, jnp.zeros_like(own_out))
    grad_local = (out_grad.astype(jnp.float32) + 0.25 * (above + own_out)).astype(jnp.bfloat16)
    grad_full = lax.all_gather(grad_local, "tensor", axis=1, tiled=True)
    d_context = jnp.dot(grad_full, o_weight[0], preferred_element_type=jnp.float32).astype(
        jnp.bfloat16
    )
    three = (rows, head_count, HD)
    query_b = queries[0].reshape(three)
    key_b = key_heads[0].reshape(three)
    value_b = values[0].reshape(three)
    dctx_b = d_context.reshape(three)
    ctx_flat = context[0]
    ends = jnp.cumsum(doc_lengths)
    first = lax.axis_index("dp") * rows
    own_place = first + jnp.arange(rows, dtype=jnp.int32)
    own_docs = document_of(own_place, ends)
    key_list = []
    value_list = []
    for step in range(REACH, 0, -1):
        moved = passed_along((key_heads[0], values[0]), "dp", step)
        key_list.append(moved[0])
        value_list.append(moved[1])
    window = (REACH + 1) * rows
    key_win = jnp.concatenate(key_list + [key_heads[0]], 0).reshape(window, head_count, HD)
    value_win = jnp.concatenate(value_list + [values[0]], 0).reshape(window, head_count, HD)
    window_place = first - REACH * rows + jnp.arange(window, dtype=jnp.int32)
    window_docs = document_of(window_place, ends)
    allowed = (
        (own_docs[:, None] == window_docs[None, :])
        & (window_place[None, :] <= own_place[:, None])
        & (window_place[None, :] >= 0)
    )
    scores = (
        jnp.einsum("ihd,jhd->hij", query_b, key_win, preferred_element_type=jnp.float32) * scaling
    )
    scores = jnp.where(allowed[None], scores, -jnp.inf)
    prob = jax.nn.softmax(scores, axis=-1)
    d_prob = jnp.einsum("ihd,jhd->hij", dctx_b, value_win, preferred_element_type=jnp.float32)
    delta = jnp.transpose(
        jnp.sum(dctx_b.astype(jnp.float32) * ctx_flat.reshape(three).astype(jnp.float32), axis=-1)
    )
    d_score = (prob * (d_prob - delta[..., None]) * scaling).astype(jnp.bfloat16)
    query_grad = jnp.einsum(
        "hij,jhd->ihd", d_score, key_win, preferred_element_type=jnp.float32
    ).astype(jnp.bfloat16)
    peak = jnp.max(scores, axis=-1)
    log_total = peak + jnp.log(jnp.sum(jnp.exp(scores - peak[..., None]), axis=-1))
    query_sets = [query_b]
    dctx_sets = [dctx_b]
    total_sets = [log_total]
    delta_sets = [delta]
    for step in range(1, REACH + 1):
        rows_in = passed_along((queries[0], d_context), "dp", -step)
        stats_in = passed_along((log_total, delta), "dp", -step)
        query_sets.append(rows_in[0].reshape(three))
        dctx_sets.append(rows_in[1].reshape(three))
        total_sets.append(stats_in[0])
        delta_sets.append(stats_in[1])
    query_set = jnp.concatenate(query_sets, 0)
    dctx_set = jnp.concatenate(dctx_sets, 0)
    total_set = jnp.concatenate(total_sets, 1)
    delta_set = jnp.concatenate(delta_sets, 1)
    set_place = first + jnp.arange(window, dtype=jnp.int32)
    set_docs = document_of(set_place, ends)
    allowed_back = (set_docs[:, None] == own_docs[None, :]) & (
        own_place[None, :] <= set_place[:, None]
    )
    back_scores = (
        jnp.einsum("ihd,jhd->hij", query_set, key_b, preferred_element_type=jnp.float32) * scaling
    )
    prob_back = jnp.exp(jnp.where(allowed_back[None], back_scores - total_set[..., None], -jnp.inf))
    prob_back_b = prob_back.astype(jnp.bfloat16)
    d_prob_back = jnp.einsum("ihd,jhd->hij", dctx_set, value_b, preferred_element_type=jnp.float32)
    d_score_back = (prob_back * (d_prob_back - delta_set[..., None]) * scaling).astype(jnp.bfloat16)
    key_sum = jnp.einsum(
        "hij,ihd->jhd", d_score_back, query_set, preferred_element_type=jnp.float32
    )
    value_sum = jnp.einsum(
        "hij,ihd->jhd", prob_back_b, dctx_set, preferred_element_type=jnp.float32
    )
    weight_grad = lax.psum_scatter(
        lax.dot_general(
            grad_full, ctx_flat, (((0,), (0,)), ((), ())), preferred_element_type=jnp.float32
        ).astype(jnp.bfloat16),
        "dp",
        scatter_dimension=0,
        tiled=True,
    ).astype(jnp.float32)
    shape_out = (1, rows, width)
    return (
        query_grad.reshape(shape_out),
        key_sum.astype(jnp.bfloat16).reshape(shape_out),
        value_sum.astype(jnp.bfloat16).reshape(shape_out),
        weight_grad[None],
    )


def solution(mesh):
    placed = (
        P("dp", "tensor"),
        P("section", "dp", "tensor"),
        P("section", "dp", "tensor"),
        P("section", "dp", "tensor"),
        P("section", "dp", "tensor"),
        P("section", "dp", "tensor"),
        P("section", None, "tensor"),
        P(),
    )
    return jax.shard_map(
        on_device,
        mesh=mesh,
        in_specs=placed,
        out_specs=(
            P("section", "dp", "tensor"),
            P("section", "dp", "tensor"),
            P("section", "dp", "tensor"),
            P("section", "dp", "tensor"),
        ),
        check_vma=False,
    )
```

profile of v0, /device:TPU:12, one launch (start us, length us, event | category | flops | bytes accessed | tf_op | source)
XLA Modules:
  0.0 265.2 jit_solution(12723246966927349011)
XLA Ops:
  8.0 24.4 %all-gather.3.cloned.1.call-done = bf16[4,128,2048]{2,1,0:T(8,128)(2,1)} async-done(((bf16[1,128,2048]{2,1,0:T(8,128)(2,1)}), bf16[4,128,2048]{2,1,0:T(8,128)(2,1)}) %all-gather.3.cloned.1.call-update) | async-done | bytes 2097168 | tf_op jit(solution)/shard_map/all_gather | solution.py:12
  32.4 6.6 %while.16 = (s32[]{:T(128)}, f32[128,2048]{1,0:T(8,128)S(1)}, s32[]{:T(128)}, bf16[4,128,2048]{2,1,0:T(8,128)(2,1)}, s32[]{:T(128)}, /*index=5*/s32[]{:T(128)}, s32[]{:T(128)}, s32[]{:T(128)}) while((s32[]{:T(128)}, f32[128,2048]{1,0:T(8,128)S(1)}, s32[]{:T(128)}, bf16[4,128,2048]{2,1,0:T(8,128)(2,1)}, s32[]{:T(128)}, ...), condition=%wide.region_6.7_spmd.clone, body=%wide.region_5.6_spmd.clone.sunk | while | flops 1048584 | bytes 2621603 | solution.py:21
  40.1 22.3 %all-gather.5.cloned.1.call-done = bf16[128,4096]{1,0:T(8,128)(2,1)} async-done(((bf16[128,2048]{1,0:T(8,128)(2,1)}), bf16[128,4096]{1,0:T(8,128)(2,1)}) %all-gather.5.cloned.1.call-update) | async-done | bytes 1048592 | tf_op jit(solution)/shard_map/all_gather | solution.py:45
  62.5 6.8 %convolution_convert_fusion = bf16[4096,1024]{1,0:T(8,128)(2,1)} fusion(bf16[128,4096]{1,0:T(8,128)(2,1)} %all-gather.5.cloned.1.call-done, bf16[1,128,1024]{2,1,0:T(8,128)(2,1)S(1)} %copy-done.6), kind=kOutput, calls=%fused_computation.3 | convolution fusion | flops 1077936128 | bytes 9699328 | tf_op jit(solution)/shard_map/dot_general | solution.py:124
  71.1 3.4 %collective-permute-start.3 = (bf16[128,1024]{0,1:T(8,128)(2,1)}, bf16[128,1024]{0,1:T(8,128)(2,1)}, u32[]{:S(2)}, u32[]{:S(2)}) collective-permute-start(bf16[128,1024]{0,1:T(8,128)(2,1)} %bitcast.10), channel_id=1, source_target_pairs={{0,2},{2,4},{4,6},{1,3},{3,5},{5,7},{8,10},{10,12},{12,14},{9,11},... | collective-permute-start | bytes 786440 | tf_op jit(solution)/shard_map/ppermute | solution.py:27
  74.5 2.9 %collective-permute-start.2 = (bf16[128,1024]{0,1:T(8,128)(2,1)}, bf16[128,1024]{0,1:T(8,128)(2,1)}, u32[]{:S(2)}, u32[]{:S(2)}) collective-permute-start(bf16[128,1024]{0,1:T(8,128)(2,1)} %bitcast.10), channel_id=1, source_target_pairs={{0,4},{2,6},{1,5},{3,7},{8,12},{10,14},{9,13},{11,15},{16,20},{18,... | collective-permute-start | bytes 786440 | tf_op jit(solution)/shard_map/ppermute | solution.py:27
  77.6 1.9 collective-permute-start.1
  84.0 1.9 copy.145
  86.2 53.4 %collective-permute-done.1 = bf16[128,1024]{0,1:T(8,128)(2,1)S(1)} collective-permute-done((bf16[128,1024]{0,1:T(8,128)(2,1)S(1)}, bf16[128,1024]{0,1:T(8,128)(2,1)S(1)}, u32[]{:S(2)}, u32[]{:S(2)}) %collective-permute-start.1) | collective-permute-done | bytes 262176 | tf_op jit(solution)/shard_map/ppermute | solution.py:27
  139.6 1.9 collective-permute-start.4
  141.7 20.0 %collective-permute-done = bf16[128,1024]{0,1:T(8,128)(2,1)S(1)} collective-permute-done((bf16[128,1024]{0,1:T(8,128)(2,1)S(1)}, bf16[128,1024]{0,1:T(8,128)(2,1)S(1)}, u32[]{:S(2)}, u32[]{:S(2)}) %collective-permute-start) | collective-permute-done | bytes 262176 | tf_op jit(solution)/shard_map/ppermute | solution.py:27
  165.3 1.9 collective-permute-start.6
  170.5 1.8 copy.144
  172.3 1.8 copy.143
  174.1 4.7 %fusion.7 = bf16[128,1024]{1,0:T(8,128)(2,1)S(1)} fusion(bf16[128,4096]{1,0:T(8,128)(2,1)S(1)} %copy-done, bf16[1,4096,1024]{2,1,0:T(8,128)(2,1)} %param.16), kind=kOutput, calls=%fused_computation.15 | convolution fusion | flops 1073872896 | bytes 9699328 | tf_op jit(solution)/shard_map/dot_general | solution.py:46
  180.4 1.9 collective-permute-start.10
  183.7 2.1 collective-permute-start.8
  185.8 2.8 %fusion.5 = bf16[8,128,128]{2,1,0:T(8,128)(2,1)S(1)} fusion(f32[8,128,384]{1,2,0:T(8,128)} %copy-done.2, bf16[128,8,128]{2,0,1:T(8,128)(2,1)} %copy.145, bf16[128,8,128]{2,0,1:T(8,128)(2,1)} %copy.144, bf16[128,8,128]{2,0,1:T(8,128)(2,1)} %copy.143, f32[8,128]{1,0:T(8,128)S(1)} %copy.147, f32[8,128]{1,0:T(8,128)S(1)} %fusion.2, ...), kind=kOutput, calls=%fused_computation.13 | convolution fusion | flops 208535552 | bytes 3682304 | tf_op jit(solution)/shard_map/hij,jhd->ihd/dot_general | solution.py:85
  190.2 9.5 %collective-permute-done.10 = f32[8,128]{0,1:T(8,128)S(1)} collective-permute-done((f32[8,128]{0,1:T(8,128)S(1)}, f32[8,128]{0,1:T(8,128)S(1)}, u32[]{:S(2)}, u32[]{:S(2)}) %collective-permute-start.10) | collective-permute-done | bytes 4128 | tf_op jit(solution)/shard_map/ppermute | solution.py:27
  199.8 38.9 %collective-permute-done.8 = bf16[128,1024]{1,0:T(8,128)(2,1)S(1)} collective-permute-done((bf16[128,1024]{1,0:T(8,128)(2,1)S(1)}, bf16[128,1024]{1,0:T(8,128)(2,1)S(1)}, u32[]{:S(2)}, u32[]{:S(2)}) %collective-permute-start.8) | collective-permute-done | bytes 262176 | tf_op jit(solution)/shard_map/ppermute | solution.py:27
  240.2 2.2 convolution_convert_fusion.1
  243.2 2.2 fusion.6
  246.4 8.2 %reduce-scatter.2.cloned.1.call-done = bf16[1024,1024]{1,0:T(8,128)(2,1)} async-done(((bf16[4096,1024]{1,0:T(8,128)(2,1)}), bf16[1024,1024]{1,0:T(8,128)(2,1)}) %reduce-scatter.2.cloned.1.call-update) | async-done | bytes 2097168 | tf_op jit(solution)/shard_map/reduce_scatter | solution.py:123
  254.6 4.1 %bitcast_convert_fusion = f32[1,1024,1024]{2,1,0:T(8,128)} fusion(bf16[1024,1024]{1,0:T(8,128)(2,1)} %reduce-scatter.2.cloned.1.call-done), kind=kLoop, calls=%fused_computation.4 | loop fusion | flops 1048576 | bytes 6291456 | tf_op jit(solution)/shard_map/broadcast_in_dim | solution.py:136
  (94 shorter events, 29.8 us)
Async XLA Ops:
  7.2 25.2 %all-gather.3.cloned.1.call-start = ((), (), s32[]{:S(2)}) async-start(), calls=%async_computation.1 | async-start | bytes 2621440 | tf_op jit(solution)/shard_map/all_gather | solution.py:12
  7.9 54.6 %all-gather.5.cloned.1.call-start = ((), (), s32[]{:S(2)}) async-start(), calls=%async_computation.2 | async-start | bytes 1572864 | tf_op jit(solution)/shard_map/all_gather | solution.py:45
  32.4 6.6 %copy-start.1 = (bf16[1,128,2048]{2,1,0:T(8,128)(2,1)S(1)}, bf16[1,128,2048]{2,1,0:T(8,128)(2,1)}, u32[]{:S(2)}) copy-start(bf16[1,128,2048]{2,1,0:T(8,128)(2,1)} %param.11) | copy-start | bytes 1572868
  32.4 6.7 %copy-start.7 = (bf16[128,2048]{1,0:T(8,128)(2,1)S(1)}, bf16[128,2048]{1,0:T(8,128)(2,1)}, u32[]{:S(2)}) copy-start(bf16[128,2048]{1,0:T(8,128)(2,1)} %param.10) | copy-start | bytes 1572868
  39.0 23.4 %copy-start.6 = (bf16[1,128,1024]{2,1,0:T(8,128)(2,1)S(1)}, bf16[1,128,1024]{2,1,0:T(8,128)(2,1)}, u32[]{:S(2)}) copy-start(bf16[1,128,1024]{2,1,0:T(8,128)(2,1)} %param.12) | copy-start | bytes 786436
  40.1 214.5 %reduce-scatter.2.cloned.1.call-start = ((), (), s32[]{:S(2)}) async-start(), calls=%async_computation.3 | async-start | bytes 10485760 | tf_op jit(solution)/shard_map/reduce_scatter | solution.py:123
  69.3 8.1 %copy-start.9 = (bf16[1,128,1024]{2,1,0:T(8,128)(2,1)S(1)}, bf16[1,128,1024]{2,1,0:T(8,128)(2,1)}, u32[]{:S(2)}) copy-start(bf16[1,128,1024]{2,1,0:T(8,128)(2,1)} %param.14) | copy-start | bytes 786436
  69.3 11.5 %copy-start.10 = (bf16[1,128,1024]{2,1,0:T(8,128)(2,1)S(1)}, bf16[1,128,1024]{2,1,0:T(8,128)(2,1)}, u32[]{:S(2)}) copy-start(bf16[1,128,1024]{2,1,0:T(8,128)(2,1)} %param.13) | copy-start | bytes 786436
  70.2 12.1 %copy-start.15 = (s32[4]{0:T(128)S(1)}, s32[4]{0:T(128)}, u32[]{:S(2)}) copy-start(s32[4]{0:T(128)} %param.17) | copy-start | bytes 52
  71.1 99.4 %collective-permute-start.3 = (bf16[128,1024]{0,1:T(8,128)(2,1)}, bf16[128,1024]{0,1:T(8,128)(2,1)}, u32[]{:S(2)}, u32[]{:S(2)}) collective-permute-start(bf16[128,1024]{0,1:T(8,128)(2,1)} %bitcast.10), channel_id=1, source_target_pairs={{0,2},{2,4},{4,6},{1,3},{3,5},{5,7},{8,10},{10,12},{12,14},{9,11},... | collective-permute-start | bytes 786440 | tf_op jit(solution)/shard_map/ppermute | solution.py:27
  74.5 97.8 %collective-permute-start.2 = (bf16[128,1024]{0,1:T(8,128)(2,1)}, bf16[128,1024]{0,1:T(8,128)(2,1)}, u32[]{:S(2)}, u32[]{:S(2)}) collective-permute-start(bf16[128,1024]{0,1:T(8,128)(2,1)} %bitcast.10), channel_id=1, source_target_pairs={{0,4},{2,6},{1,5},{3,7},{8,12},{10,14},{9,13},{11,15},{16,20},{18,... | collective-permute-start | bytes 786440 | tf_op jit(solution)/shard_map/ppermute | solution.py:27
  77.6 62.0 %collective-permute-start.1 = (bf16[128,1024]{0,1:T(8,128)(2,1)S(1)}, bf16[128,1024]{0,1:T(8,128)(2,1)S(1)}, u32[]{:S(2)}, u32[]{:S(2)}) collective-permute-start(bf16[128,1024]{0,1:T(8,128)(2,1)S(1)} %bitcast.81), channel_id=1, source_target_pairs={{0,2},{2,4},{4,6},{1,3},{3,5},{5,7},{8,10},{10,12},{12,14},{9,11},... | collective-permute-start | bytes 786440 | tf_op jit(solution)/shard_map/ppermute | solution.py:27
  79.5 82.2 %collective-permute-start = (bf16[128,1024]{0,1:T(8,128)(2,1)S(1)}, bf16[128,1024]{0,1:T(8,128)(2,1)S(1)}, u32[]{:S(2)}, u32[]{:S(2)}) collective-permute-start(bf16[128,1024]{0,1:T(8,128)(2,1)S(1)} %bitcast.82), channel_id=1, source_target_pairs={{0,4},{2,6},{1,5},{3,7},{8,12},{10,14},{9,13},{11,15},{16,20},{18,... | collective-permute-start | bytes 786440 | tf_op jit(solution)/shard_map/ppermute | solution.py:27
  81.0 84.3 %collective-permute-start.5 = (bf16[128,1024]{0,1:T(8,128)(2,1)S(1)}, bf16[128,1024]{0,1:T(8,128)(2,1)S(1)}, u32[]{:S(2)}, u32[]{:S(2)}) collective-permute-start(bf16[128,1024]{0,1:T(8,128)(2,1)S(1)} %bitcast.86), channel_id=1, source_target_pairs={{4,0},{6,2},{5,1},{7,3},{12,8},{14,10},{13,9},{15,11},{20,16},{22,... | collective-permute-start | bytes 786440 | tf_op jit(solution)/shard_map/ppermute | solution.py:27
  83.9 78.3 %copy-start.11 = (bf16[128,8,128]{2,0,1:T(8,128)(2,1)}, bf16[128,8,128]{2,0,1:T(8,128)(2,1)S(1)}, u32[]{:S(2)}) copy-start(bf16[128,8,128]{2,0,1:T(8,128)(2,1)S(1)} %copy.138) | copy-start | bytes 786436
  139.6 28.4 %collective-permute-start.4 = (bf16[128,1024]{0,1:T(8,128)(2,1)S(1)}, bf16[128,1024]{0,1:T(8,128)(2,1)S(1)}, u32[]{:S(2)}, u32[]{:S(2)}) collective-permute-start(bf16[128,1024]{0,1:T(8,128)(2,1)S(1)} %bitcast.88), channel_id=1, source_target_pairs={{2,0},{4,2},{6,4},{3,1},{5,3},{7,5},{10,8},{12,10},{14,12},{11,9},... | collective-permute-start | bytes 786440 | tf_op jit(solution)/shard_map/ppermute | solution.py:27
  141.7 20.5 %copy-start.12 = (bf16[128,8,128]{2,0,1:T(8,128)(2,1)}, bf16[128,8,128]{2,0,1:T(8,128)(2,1)S(1)}, u32[]{:S(2)}) copy-start(bf16[128,8,128]{2,0,1:T(8,128)(2,1)S(1)} %copy.137) | copy-start | bytes 786436
  164.0 10.1 %collective-permute-start.7 = (f32[8,128]{1,0:T(8,128)S(1)}, f32[8,128]{1,0:T(8,128)S(1)}, u32[]{:S(2)}, u32[]{:S(2)}) collective-permute-start(f32[8,128]{1,0:T(8,128)S(1)} %log_add_fusion), channel_id=1, source_target_pairs={{4,0},{6,2},{5,1},{7,3},{12,8},{14,10},{13,9},{15,11},{20,16},{22,... | collective-permute-start | bytes 12296 | tf_op jit(solution)/shard_map/ppermute | solution.py:27
  165.3 8.8 %collective-permute-start.6 = (f32[8,128]{1,0:T(8,128)S(1)}, f32[8,128]{1,0:T(8,128)S(1)}, u32[]{:S(2)}, u32[]{:S(2)}) collective-permute-start(f32[8,128]{1,0:T(8,128)S(1)} %log_add_fusion), channel_id=1, source_target_pairs={{2,0},{4,2},{6,4},{3,1},{5,3},{7,5},{10,8},{12,10},{14,12},{11,9},... | collective-permute-start | bytes 12296 | tf_op jit(solution)/shard_map/ppermute | solution.py:27
  168.9 5.2 %copy-start = (bf16[128,4096]{1,0:T(8,128)(2,1)S(1)}, bf16[128,4096]{1,0:T(8,128)(2,1)}, u32[]{:S(2)}) copy-start(bf16[128,4096]{1,0:T(8,128)(2,1)} %all-gather.5.cloned.1.call-done) | copy-start | bytes 3145732
  179.1 11.0 %collective-permute-start.11 = (f32[8,128]{0,1:T(8,128)S(1)}, f32[8,128]{0,1:T(8,128)S(1)}, u32[]{:S(2)}, u32[]{:S(2)}) collective-permute-start(f32[8,128]{0,1:T(8,128)S(1)} %bitcast.99), channel_id=1, source_target_pairs={{4,0},{6,2},{5,1},{7,3},{12,8},{14,10},{13,9},{15,11},{20,16},{22,... | collective-permute-start | bytes 12296 | tf_op jit(solution)/shard_map/ppermute | solution.py:27
  180.4 19.3 %collective-permute-start.10 = (f32[8,128]{0,1:T(8,128)S(1)}, f32[8,128]{0,1:T(8,128)S(1)}, u32[]{:S(2)}, u32[]{:S(2)}) collective-permute-start(f32[8,128]{0,1:T(8,128)S(1)} %bitcast.100), channel_id=1, source_target_pairs={{2,0},{4,2},{6,4},{3,1},{5,3},{7,5},{10,8},{12,10},{14,12},{11,9},... | collective-permute-start | bytes 12296 | tf_op jit(solution)/shard_map/ppermute | solution.py:27
  182.4 57.1 %collective-permute-start.9 = (bf16[128,1024]{1,0:T(8,128)(2,1)S(1)}, bf16[128,1024]{1,0:T(8,128)(2,1)S(1)}, u32[]{:S(2)}, u32[]{:S(2)}) collective-permute-start(bf16[128,1024]{1,0:T(8,128)(2,1)S(1)} %fusion.7), channel_id=1, source_target_pairs={{4,0},{6,2},{5,1},{7,3},{12,8},{14,10},{13,9},{15,11},{20,16},{22,... | collective-permute-start | bytes 786440 | tf_op jit(solution)/shard_map/ppermute | solution.py:27
  183.7 55.0 %collective-permute-start.8 = (bf16[128,1024]{1,0:T(8,128)(2,1)S(1)}, bf16[128,1024]{1,0:T(8,128)(2,1)S(1)}, u32[]{:S(2)}, u32[]{:S(2)}) collective-permute-start(bf16[128,1024]{1,0:T(8,128)(2,1)S(1)} %fusion.7), channel_id=1, source_target_pairs={{2,0},{4,2},{6,4},{3,1},{5,3},{7,5},{10,8},{12,10},{14,12},{11,9},... | collective-permute-start | bytes 786440 | tf_op jit(solution)/shard_map/ppermute | solution.py:27
  (7 other events, 15.0 us)
Sparse Core Ops, SparseCore 0:
  9.6 22.7 all-gather.2
  40.2 22.2 all-gather.4
  69.4 185.0 reduce-scatter.1
where the time goes:
time: 266 us; the launch traced here: 265 us
  waiting for transfers between devices  177 us (67%)
  starting transfers between devices  22.7 us (9%)
  matrix products  20.7 us (8%)
  local copies, waits for them, and re-layouts  17.3 us (7%)
  between operations  14.1 us (5%)
  other arithmetic  12.9 us (5%)
    ppermute x12, waiting for transfers between devices, passed_along(): lax.ppermute(value, axis, [(source, source + steps) for source in range(l...  122 us
    all_gather x1, waiting for transfers between devices, entering(): everything = lax.all_gather(value.astype(jnp.bfloat16), axis)  24.4 us
    ppermute x12, starting transfers between devices, passed_along(): lax.ppermute(value, axis, [(source, source + steps) for source in range(l...  22.6 us
    all_gather x1, waiting for transfers between devices, on_device(): grad_full = lax.all_gather(grad_local, 'tensor', axis=1, tiled=True)  22.3 us
    reduce_scatter x1, waiting for transfers between devices, on_device(): lax.psum_scatter(lax.dot_general(grad_full, ctx_flat, (((0,), (0,)), ((),...  8.21 us
    unnamed x42, local copies, waits for them, and re-layouts  7.8 us
    dot_general x1, matrix products, on_device(): lax.dot_general(grad_full, ctx_flat, (((0,), (0,)), ((), ())), preferred_...  6.83 us
    select_n x4, other arithmetic, hop(): return jnp.where(reached, new, before)  6.55 us
  transfers between devices with their start and end apart: 15, of which 7 were waited for; matrix products, arithmetic and copies ran while one was open for 11% of the time, Pallas kernels for 0%

commit v1 on v0

v1 whole, which is shorter than its diff:
```python
import jax
import jax.numpy as jnp
from jax import lax
from jax.sharding import PartitionSpec as P

HD = 128
REACH = 2


def passed_along(value, axis, steps):
    count = lax.axis_size(axis)
    leading, last = (max(0, -steps), min(count, count - steps))
    return lax.ppermute(value, axis, [(source, source + steps) for source in range(leading, last)])


def suffix_sum(own, axis):
    count = lax.axis_size(axis)
    total = own.astype(jnp.float32)
    step = 1
    while step < count:
        total = total + passed_along(total.astype(jnp.bfloat16), axis, -step).astype(jnp.float32)
        step *= 2
    return total


def document_of(positions, ends):
    return jnp.sum((positions[:, None] >= ends[None, :]).astype(jnp.int32), axis=-1)


def on_device(out_grad, section_out, context, queries, key_heads, values, o_weight, doc_lengths):
    rows, width = (queries.shape[1], queries.shape[2])
    head_count = width // HD
    scaling = HD ** (-0.5)
    n_dp, n_tensor = lax.axis_size("dp"), lax.axis_size("tensor")
    dp_at, tensor_at = lax.axis_index("dp"), lax.axis_index("tensor")
    docs = doc_lengths.shape[0]
    ends = jnp.sum(
        jnp.where(jnp.arange(docs)[:, None] >= jnp.arange(docs)[None, :], doc_lengths[None, :], 0),
        axis=1,
    )
    three = (rows, head_count, HD)
    first = dp_at * rows
    own_place = first + jnp.arange(rows, dtype=jnp.int32)
    own_docs = document_of(own_place, ends)
    window = (REACH + 1) * rows

    upper = suffix_sum(section_out[0], "section")
    grad_local = (out_grad.astype(jnp.float32) + 0.25 * upper).astype(jnp.bfloat16)

    kv = jnp.concatenate([key_heads[0], values[0]], 1)
    kv_sets, query_flat = [kv], [queries[0]]
    for step in range(REACH):
        kv_sets.append(passed_along(kv_sets[-1], "dp", 1))
        query_flat.append(passed_along(query_flat[-1], "dp", -1))
    context_all = lax.all_gather(context[0], "dp", axis=0, tiled=True)

    local_width = grad_local.shape[1]
    grad_full = jnp.zeros((rows, local_width * n_tensor), jnp.bfloat16)
    d_context = jnp.zeros((rows, width), jnp.float32)
    for step in range(n_tensor):
        part = grad_local
        if step:
            part = lax.ppermute(
                grad_local, "tensor", [(i, (i + step) % n_tensor) for i in range(n_tensor)]
            )
        start = lax.rem(tensor_at + n_tensor - step, n_tensor) * local_width
        grad_full = lax.dynamic_update_slice_in_dim(grad_full, part, start, 1)
        weight = lax.dynamic_slice_in_dim(o_weight[0], start, local_width, 0)
        d_context = d_context + jnp.dot(part, weight, preferred_element_type=jnp.float32)
    d_context = d_context.astype(jnp.bfloat16)
    dctx_flat = [d_context]
    for step in range(REACH):
        dctx_flat.append(passed_along(dctx_flat[-1], "dp", -1))
    grad_blocks = lax.all_to_all(grad_full, "dp", split_axis=1, concat_axis=0, tiled=True)

    query_b = queries[0].reshape(three)
    key_b = key_heads[0].reshape(three)
    value_b = values[0].reshape(three)
    dctx_b = d_context.reshape(three)
    kv_win = jnp.concatenate(kv_sets[::-1], 0)
    key_win = kv_win[:, :width].reshape(window, head_count, HD)
    value_win = kv_win[:, width:].reshape(window, head_count, HD)
    window_place = first - REACH * rows + jnp.arange(window, dtype=jnp.int32)
    window_docs = document_of(window_place, ends)
    allowed = (
        (own_docs[:, None] == window_docs[None, :])
        & (window_place[None, :] <= own_place[:, None])
        & (window_place[None, :] >= 0)
    )
    scores = (
        jnp.einsum("ihd,jhd->hij", query_b, key_win, preferred_element_type=jnp.float32) * scaling
    )
    scores = jnp.where(allowed[None], scores, -jnp.inf)
    peak = jnp.max(scores, axis=-1)
    log_total = peak + jnp.log(jnp.sum(jnp.exp(scores - peak[..., None]), axis=-1))
    total_sets = [log_total]
    for step in range(REACH):
        total_sets.append(passed_along(total_sets[-1], "dp", -1))
    prob = jnp.exp(scores - log_total[..., None])
    d_prob = jnp.einsum("ihd,jhd->hij", dctx_b, value_win, preferred_element_type=jnp.float32)

    dctx_set = jnp.concatenate(dctx_flat, 0).reshape(window, head_count, HD)
    padded = jnp.concatenate([context_all, jnp.zeros((REACH * rows, width), context_all.dtype)], 0)
    context_set = lax.dynamic_slice_in_dim(padded, first, window, 0)
    delta_set = jnp.transpose(
        jnp.sum(
            dctx_set.astype(jnp.float32)
            * context_set.reshape(window, head_count, HD).astype(jnp.float32),
            axis=-1,
        )
    )
    delta = jnp.transpose(
        jnp.sum(dctx_b.astype(jnp.float32) * context[0].reshape(three).astype(jnp.float32), axis=-1)
    )
    d_score = (prob * (d_prob - delta[..., None]) * scaling).astype(jnp.bfloat16)
    query_grad = jnp.einsum(
        "hij,jhd->ihd", d_score, key_win, preferred_element_type=jnp.float32
    ).astype(jnp.bfloat16)

    query_set = jnp.concatenate(query_flat, 0).reshape(window, head_count, HD)
    total_set = jnp.concatenate(total_sets, 1)
    set_place = first + jnp.arange(window, dtype=jnp.int32)
    set_docs = document_of(set_place, ends)
    allowed_back = (
        (set_docs[:, None] == own_docs[None, :])
        & (own_place[None, :] <= set_place[:, None])
        & (set_place[:, None] < n_dp * rows)
    )
    back_scores = (
        jnp.einsum("ihd,jhd->hij", query_set, key_b, preferred_element_type=jnp.float32) * scaling
    )
    prob_back = jnp.exp(jnp.where(allowed_back[None], back_scores - total_set[..., None], -jnp.inf))
    d_prob_back = jnp.einsum("ihd,jhd->hij", dctx_set, value_b, preferred_element_type=jnp.float32)
    d_score_back = (prob_back * (d_prob_back - delta_set[..., None]) * scaling).astype(jnp.bfloat16)
    key_sum = jnp.einsum(
        "hij,ihd->jhd", d_score_back, query_set, preferred_element_type=jnp.float32
    )
    value_sum = jnp.einsum(
        "hij,ihd->jhd",
        prob_back.astype(jnp.bfloat16),
        dctx_set,
        preferred_element_type=jnp.float32,
    )
    weight_grad = lax.dot_general(
        grad_blocks, context_all, (((0,), (0,)), ((), ())), preferred_element_type=jnp.float32
    )
    shape_out = (1, rows, width)
    return (
        query_grad.reshape(shape_out),
        key_sum.astype(jnp.bfloat16).reshape(shape_out),
        value_sum.astype(jnp.bfloat16).reshape(shape_out),
        weight_grad[None],
    )


def solution(mesh):
    placed = (
        P("dp", "tensor"),
        P("section", "dp", "tensor"),
        P("section", "dp", "tensor"),
        P("section", "dp", "tensor"),
        P("section", "dp", "tensor"),
        P("section", "dp", "tensor"),
        P("section", None, "tensor"),
        P(),
    )
    return jax.shard_map(
        on_device,
        mesh=mesh,
        in_specs=placed,
        out_specs=(
            P("section", "dp", "tensor"),
            P("section", "dp", "tensor"),
            P("section", "dp", "tensor"),
            P("section", "dp", "tensor"),
        ),
        check_vma=False,
    )
```

time: 266 us -> 140 us (0.53)
  waiting for transfers between devices: 177 us -> 43.9 us
  starting transfers between devices: 22.7 us -> 35.1 us
  matrix products: 20.7 us -> 16 us
    ppermute x12 -> x10, waiting for transfers between devices: 122 us -> 43.8 us  [passed_along(): lax.ppermute(value, axis, [(source, source + steps) for source in range(l...]
    all_gather x2 -> x1, waiting for transfers between devices: 46.7 us -> 0.01 us  [on_device(): context_all = lax.all_gather(context[0], 'dp', axis=0, tiled=True)]
    reduce_scatter x1 -> x0, waiting for transfers between devices: 8.21 us -> none  [on_device(): lax.psum_scatter(lax.dot_general(grad_full, ctx_flat, (((0,), (0,)), ((),...]
    all_to_all x0 -> x1, starting transfers between devices: none -> 7.12 us  [on_device(): lax.all_to_all(grad_full, 'dp', split_axis=1, concat_axis=0, tiled=True)]
    select_n x4 -> x0, other arithmetic: 6.55 us -> none  [hop(): return jnp.where(reached, new, before)]
    dot_general x3 -> x4, matrix products: 13.7 us -> 7.59 us  [the longest x1 3.3 us: on_device(): lax.dot_general(grad_blocks, context_all, (((0,), (0,)), ((), ())), prefe...]
    concatenate x7 -> x2, local copies, waits for them, and re-layouts: 6.76 us -> 2.64 us  [on_device(): query_set = jnp.concatenate(query_flat, 0).reshape(window, head_count, HD)]
    broadcast_in_dim x1 -> x0, other arithmetic: 4.07 us -> none  [on_device(): weight_grad[None]]
  transfers between devices with their start and end apart: 15 -> 13, of which waited for: 7 -> 6; matrix products, arithmetic and copies ran while one was open for 11% -> 28% of each run, Pallas kernels for 0% -> 0%
where the time goes in v1:
time: 140 us; the launch traced here: 139 us
  waiting for transfers between devices  43.9 us (31%)
  starting transfers between devices  35.1 us (25%)
  local copies, waits for them, and re-layouts  19.1 us (14%)
  matrix products  16 us (11%)
  between operations  14.5 us (10%)
  other arithmetic  10.9 us (8%)
    ppermute x10, waiting for transfers between devices, passed_along(): lax.ppermute(value, axis, [(source, source + steps) for source in range(l...  43.8 us
    ppermute x10, starting transfers between devices, passed_along(): lax.ppermute(value, axis, [(source, source + steps) for source in range(l...  26.4 us
    unnamed x50, local copies, waits for them, and re-layouts  11.4 us
    all_to_all x1, starting transfers between devices, on_device(): lax.all_to_all(grad_full, 'dp', split_axis=1, concat_axis=0, tiled=True)  7.12 us
    dot_general x1, matrix products, on_device(): jnp.einsum('hij,ihd->jhd', d_score_back, query_set, preferred_element_typ...  3.71 us
    dot_general x1, matrix products, on_device(): lax.dot_general(grad_blocks, context_all, (((0,), (0,)), ((), ())), prefe...  3.3 us
  transfers between devices with their start and end apart: 13, of which 6 were waited for; matrix products, arithmetic and copies ran while one was open for 28% of the time, Pallas kernels for 0%

profile of v1, /device:TPU:12, one launch (start us, length us, event | category | flops | bytes accessed | tf_op | source)
XLA Modules:
  0.0 139.5 jit_solution(8848239091446203357)
XLA Ops:
  10.4 3.5 %collective-permute-start = (bf16[128,2048]{0,1:T(8,128)(2,1)}, bf16[128,2048]{0,1:T(8,128)(2,1)}, u32[]{:S(2)}, u32[]{:S(2)}) collective-permute-start(bf16[128,2048]{0,1:T(8,128)(2,1)} %pad_maximum_fusion.1), channel_id=1, source_target_pairs={{0,2},{2,4},{4,6},{1,3},{3,5},{5,7},{8,10},{10,12},{12,14},{9,11},... | collective-permute-start | bytes 1572872 | tf_op jit(solution)/shard_map/ppermute | solution.py:13
  14.2 2.1 %collective-permute-start.2 = (bf16[128,2048]{0,1:T(8,128)(2,1)S(1)}, bf16[128,2048]{0,1:T(8,128)(2,1)S(1)}, u32[]{:S(2)}, u32[]{:S(2)}) collective-permute-start(bf16[128,2048]{0,1:T(8,128)(2,1)S(1)} %bitcast.84), channel_id=1, source_target_pairs={{8,0},{16,8},{24,16},{9,1},{17,9},{25,17},{10,2},{18,10},{26,18},{... | collective-permute-start | bytes 1572872 | tf_op jit(solution)/shard_map/ppermute | solution.py:13
  16.4 3.2 %collective-permute-start.5 = (bf16[128,1024]{0,1:T(8,128)(2,1)S(1)}, bf16[128,1024]{0,1:T(8,128)(2,1)}, u32[]{:S(2)}, u32[]{:S(2)}) collective-permute-start(bf16[128,1024]{0,1:T(8,128)(2,1)S(1)} %bitcast.93), channel_id=1, source_target_pairs={{2,0},{4,2},{6,4},{3,1},{5,3},{7,5},{10,8},{12,10},{14,12},{11,9},... | collective-permute-start | bytes 786440 | tf_op jit(solution)/shard_map/ppermute | solution.py:13
  20.3 6.0 %collective-permute-done = bf16[128,2048]{0,1:T(8,128)(2,1)} collective-permute-done((bf16[128,2048]{0,1:T(8,128)(2,1)}, bf16[128,2048]{0,1:T(8,128)(2,1)}, u32[]{:S(2)}, u32[]{:S(2)}) %collective-permute-start) | collective-permute-done | bytes 524320 | tf_op jit(solution)/shard_map/ppermute | solution.py:13
  26.3 3.5 %collective-permute-start.1 = (bf16[128,2048]{0,1:T(8,128)(2,1)}, bf16[128,2048]{0,1:T(8,128)(2,1)}, u32[]{:S(2)}, u32[]{:S(2)}) collective-permute-start(bf16[128,2048]{0,1:T(8,128)(2,1)} %collective-permute-done), channel_id=1, source_target_pairs={{0,2},{2,4},{4,6},{1,3},{3,5},{5,7},{8,10},{10,12},{12,14},{9,11},... | collective-permute-start | bytes 1572872 | tf_op jit(solution)/shard_map/ppermute | solution.py:13
  33.5 1.8 %copy.123 = bf16[128,8,128]{2,0,1:T(8,128)(2,1)} copy(bf16[128,8,128]{0,2,1:T(8,128)(2,1)} %bitcast.13) | data formatting | bytes 524288 | tf_op jit(solution)/shard_map/concatenate | solution.py:120
  35.3 3.2 %collective-permute-start.6 = (bf16[128,1024]{0,1:T(8,128)(2,1)}, bf16[128,1024]{0,1:T(8,128)(2,1)S(1)}, u32[]{:S(2)}, u32[]{:S(2)}) collective-permute-start(bf16[128,1024]{0,1:T(8,128)(2,1)} %collective-permute-done.5), channel_id=1, source_target_pairs={{2,0},{4,2},{6,4},{3,1},{5,3},{7,5},{10,8},{12,10},{14,12},{11,9},... | collective-permute-start | bytes 786440 | tf_op jit(solution)/shard_map/ppermute | solution.py:13
  39.4 3.2 %collective-permute-start.3 = (bf16[128,2048]{0,1:T(8,128)(2,1)}, bf16[128,2048]{0,1:T(8,128)(2,1)}, u32[]{:S(2)}, u32[]{:S(2)}) collective-permute-start(bf16[128,2048]{0,1:T(8,128)(2,1)} %fusion.17), channel_id=1, source_target_pairs={{16,0},{24,8},{17,1},{25,9},{18,2},{26,10},{19,3},{27,11},{20,4},{... | collective-permute-start | bytes 1572872 | tf_op jit(solution)/shard_map/ppermute | solution.py:13
  42.6 8.4 %collective-permute-done.6 = bf16[128,1024]{0,1:T(8,128)(2,1)S(1)} collective-permute-done((bf16[128,1024]{0,1:T(8,128)(2,1)}, bf16[128,1024]{0,1:T(8,128)(2,1)S(1)}, u32[]{:S(2)}, u32[]{:S(2)}) %collective-permute-start.6) | collective-permute-done | bytes 262176 | tf_op jit(solution)/shard_map/ppermute | solution.py:13
  51.9 5.3 %collective-permute-done.1 = bf16[128,2048]{0,1:T(8,128)(2,1)} collective-permute-done((bf16[128,2048]{0,1:T(8,128)(2,1)}, bf16[128,2048]{0,1:T(8,128)(2,1)}, u32[]{:S(2)}, u32[]{:S(2)}) %collective-permute-start.1) | collective-permute-done | bytes 524320 | tf_op jit(solution)/shard_map/ppermute | solution.py:13
  63.8 1.9 %collective-permute-start.7 = (f32[8,128]{1,0:T(8,128)S(1)}, f32[8,128]{1,0:T(8,128)S(1)}, u32[]{:S(2)}, u32[]{:S(2)}) collective-permute-start(f32[8,128]{1,0:T(8,128)S(1)} %log_add_fusion), channel_id=1, source_target_pairs={{2,0},{4,2},{6,4},{3,1},{5,3},{7,5},{10,8},{12,10},{14,12},{11,9},... | collective-permute-start | bytes 12296 | tf_op jit(solution)/shard_map/ppermute | solution.py:13
  67.3 2.5 %collective-permute-done.7 = f32[8,128]{1,0:T(8,128)S(1)} collective-permute-done((f32[8,128]{1,0:T(8,128)S(1)}, f32[8,128]{1,0:T(8,128)S(1)}, u32[]{:S(2)}, u32[]{:S(2)}) %collective-permute-start.7) | collective-permute-done | bytes 4128 | tf_op jit(solution)/shard_map/ppermute | solution.py:13
  69.8 1.9 %collective-permute-start.8 = (f32[8,128]{1,0:T(8,128)S(1)}, f32[8,128]{1,0:T(8,128)S(1)}, u32[]{:S(2)}, u32[]{:S(2)}) collective-permute-start(f32[8,128]{1,0:T(8,128)S(1)} %collective-permute-done.7), channel_id=1, source_target_pairs={{2,0},{4,2},{6,4},{3,1},{5,3},{7,5},{10,8},{12,10},{14,12},{11,9},... | collective-permute-start | bytes 12296 | tf_op jit(solution)/shard_map/ppermute | solution.py:13
  72.5 2.8 %collective-permute-done.8 = f32[8,128]{1,0:T(8,128)S(1)} collective-permute-done((f32[8,128]{1,0:T(8,128)S(1)}, f32[8,128]{1,0:T(8,128)S(1)}, u32[]{:S(2)}, u32[]{:S(2)}) %collective-permute-start.8) | collective-permute-done | bytes 4128 | tf_op jit(solution)/shard_map/ppermute | solution.py:13
  76.7 1.9 %collective-permute-start.9 = (bf16[128,1024]{1,0:T(8,128)(2,1)}, bf16[128,1024]{1,0:T(8,128)(2,1)}, u32[]{:S(2)}, u32[]{:S(2)}) collective-permute-start(bf16[128,1024]{1,0:T(8,128)(2,1)} %fusion.13), channel_id=1, source_target_pairs={{2,0},{4,2},{6,4},{3,1},{5,3},{7,5},{10,8},{12,10},{14,12},{11,9},... | collective-permute-start | bytes 786440 | tf_op jit(solution)/shard_map/ppermute | solution.py:13
  78.7 1.9 %copy.142 = bf16[16,8,8,128]{3,2,1,0:T(8,128)(2,1)} copy(bf16[16,8,8,128]{3,1,2,0:T(8,128)(2,1)} %bitcast.30) | data formatting | bytes 524288
  80.6 7.1 %all-to-all-start = ((bf16[128,4,1024]{0,2,1:T(8,128)(2,1)}), bf16[128,4,1024]{0,2,1:T(8,128)(2,1)S(1)}, u32[]{:S(2)}, u32[]{:S(2)}) async-start(bf16[128,4,1024]{0,2,1:T(8,128)(2,1)} %bitcast.86), calls=%async_computation | async-start | bytes 2097152 | tf_op jit(solution)/shard_map/all_to_all | solution.py:74
  89.1 2.1 %collective-permute-start.10 = (bf16[128,1024]{1,0:T(8,128)(2,1)}, bf16[128,1024]{1,0:T(8,128)(2,1)}, u32[]{:S(2)}, u32[]{:S(2)}) collective-permute-start(bf16[128,1024]{1,0:T(8,128)(2,1)} %collective-permute-done.9), channel_id=1, source_target_pairs={{2,0},{4,2},{6,4},{3,1},{5,3},{7,5},{10,8},{12,10},{14,12},{11,9},... | collective-permute-start | bytes 786440 | tf_op jit(solution)/shard_map/ppermute | solution.py:13
  91.2 2.7 %fusion.12 = bf16[8,128,128]{2,1,0:T(8,128)(2,1)} fusion(bf16[384,8,128]{0,2,1:T(8,128)(2,1)S(1)} %bitcast.88, f32[8,128,384]{1,2,0:T(8,128)S(1)} %get-tuple-element.35, bf16[384,8,128]{0,2,1:T(8,128)(2,1)} %bitcast.103, f32[8,128]{1,0:T(8,128)S(1)} %copy.118, f32[8,128]{1,0:T(8,128)S(1)} %log_add_fusion, bf16[128,1024]{1,0:T(8,128)(2,1)} %fusion.13), kind=kOutput, calls=%fused_computation.20 | convolution fusion | flops 203423744 | bytes 3678208 | tf_op jit(solution)/shard_map/hij,jhd->ihd/dot_general | solution.py:116
  94.0 1.8 %copy.132 = bf16[1,128,1024]{2,1,0:T(8,128)(2,1)} copy(bf16[1,128,1024]{1,2,0:T(8,128)(2,1)} %bitcast.107) | data formatting | bytes 524288
  97.5 18.9 %collective-permute-done.10 = bf16[128,1024]{1,0:T(8,128)(2,1)} collective-permute-done((bf16[128,1024]{1,0:T(8,128)(2,1)}, bf16[128,1024]{1,0:T(8,128)(2,1)}, u32[]{:S(2)}, u32[]{:S(2)}) %collective-permute-start.10) | collective-permute-done | bytes 262176 | tf_op jit(solution)/shard_map/ppermute | solution.py:13
  121.3 3.7 %fusion.11 = bf16[8,128,128]{2,1,0:T(8,128)(2,1)S(1)} fusion(bf16[384,8,128]{0,2,1:T(8,128)(2,1)} %copy.130, f32[8,384,128]{2,1,0:T(8,128)} %fusion.31, f32[8,384]{1,0:T(8,128)S(1)} %copy.128, f32[8,384]{1,0:T(8,128)S(1)} %pad_maximum_fusion.4, pred[384,128]{1,0:T(8,128)(4,1)S(1)} %and_and_fusion, bf16[128,8,128]{2,0,1:T(8,128)(2,1)} %copy.124, ...), kind=kOutput, calls=%fused_computation.19 | convolution fusion | flops 206569472 | bytes 3743744 | tf_op jit(solution)/shard_map/hij,ihd->jhd/dot_general | solution.py:135
  125.8 2.1 %convolution_convert_fusion = bf16[8,128,128]{2,1,0:T(8,128)(2,1)S(1)} fusion(bf16[384,8,128]{0,2,1:T(8,128)(2,1)S(1)} %copy-done.7, f32[8,384,128]{2,1,0:T(8,128)} %fusion.31, f32[8,384]{1,0:T(8,128)S(1)} %pad_maximum_fusion.4, pred[384,128]{1,0:T(8,128)(4,1)S(1)} %and_and_fusion), kind=kOutput, calls=%fused_computation.21 | convolution fusion | flops 102367232 | bytes 2682880 | tf_op jit(solution)/shard_map/hij,ihd->jhd/dot_general | solution.py:138
  129.3 3.3 %convolution_bitcast_fusion = f32[1,1024,1024]{2,1,0:T(8,128)} fusion(bf16[512,1024]{1,0:T(8,128)(2,1)S(1)} %bitcast.98, bf16[1,512,1024]{2,1,0:T(8,128)(2,1)S(1)} %copy-done.4), kind=kOutput, calls=%fused_computation.6 | convolution fusion | flops 1073741824 | bytes 6291456 | tf_op jit(solution)/shard_map/dot_general | solution.py:144
  (94 shorter events, 30.3 us)
Async XLA Ops:
  7.2 6.7 %copy-start.8 = (bf16[1,128,2048]{2,1,0:T(8,128)(2,1)S(1)}, bf16[1,128,2048]{2,1,0:T(8,128)(2,1)}, u32[]{:S(2)}) copy-start(bf16[1,128,2048]{2,1,0:T(8,128)(2,1)} %param.9) | copy-start | bytes 1572868
  7.2 9.1 %copy-start.10 = (bf16[1,128,1024]{2,1,0:T(8,128)(2,1)S(1)}, bf16[1,128,1024]{2,1,0:T(8,128)(2,1)}, u32[]{:S(2)}) copy-start(bf16[1,128,1024]{2,1,0:T(8,128)(2,1)} %param.11) | copy-start | bytes 786436
  7.2 88.6 %all-gather.3.cloned.1.call-start = ((), (), s32[]{:S(2)}) async-start(), calls=%async_computation.1 | async-start | bytes 1310720 | tf_op jit(solution)/shard_map/all_gather | solution.py:55
  9.5 10.2 %copy-start.15 = (s32[4]{0:T(128)S(1)}, s32[4]{0:T(128)}, u32[]{:S(2)}) copy-start(s32[4]{0:T(128)} %param.15) | copy-start | bytes 52
  9.6 10.4 %copy-start.3 = (bf16[1,128,1024]{2,1,0:T(8,128)(2,1)S(1)}, bf16[1,128,1024]{2,1,0:T(8,128)(2,1)}, u32[]{:S(2)}) copy-start(bf16[1,128,1024]{2,1,0:T(8,128)(2,1)} %param.10) | copy-start | bytes 786436
  10.4 15.9 %collective-permute-start = (bf16[128,2048]{0,1:T(8,128)(2,1)}, bf16[128,2048]{0,1:T(8,128)(2,1)}, u32[]{:S(2)}, u32[]{:S(2)}) collective-permute-start(bf16[128,2048]{0,1:T(8,128)(2,1)} %pad_maximum_fusion.1), channel_id=1, source_target_pairs={{0,2},{2,4},{4,6},{1,3},{3,5},{5,7},{8,10},{10,12},{12,14},{9,11},... | collective-permute-start | bytes 1572872 | tf_op jit(solution)/shard_map/ppermute | solution.py:13
  14.2 16.7 %copy-start.9 = (bf16[128,2048]{1,0:T(8,128)(2,1)S(1)}, bf16[128,2048]{1,0:T(8,128)(2,1)}, u32[]{:S(2)}) copy-start(bf16[128,2048]{1,0:T(8,128)(2,1)} %param.8) | copy-start | bytes 1572868
  14.2 24.3 %collective-permute-start.2 = (bf16[128,2048]{0,1:T(8,128)(2,1)S(1)}, bf16[128,2048]{0,1:T(8,128)(2,1)S(1)}, u32[]{:S(2)}, u32[]{:S(2)}) collective-permute-start(bf16[128,2048]{0,1:T(8,128)(2,1)S(1)} %bitcast.84), channel_id=1, source_target_pairs={{8,0},{16,8},{24,16},{9,1},{17,9},{25,17},{10,2},{18,10},{26,18},{... | collective-permute-start | bytes 1572872 | tf_op jit(solution)/shard_map/ppermute | solution.py:13
  16.4 14.7 %copy-start.1 = (bf16[1,128,1024]{1,2,0:T(8,128)(2,1)}, bf16[1,128,1024]{1,2,0:T(8,128)(2,1)S(1)}, u32[]{:S(2)}) copy-start(bf16[1,128,1024]{1,2,0:T(8,128)(2,1)S(1)} %copy.111) | copy-start | bytes 786436
  16.4 17.1 %collective-permute-start.5 = (bf16[128,1024]{0,1:T(8,128)(2,1)S(1)}, bf16[128,1024]{0,1:T(8,128)(2,1)}, u32[]{:S(2)}, u32[]{:S(2)}) collective-permute-start(bf16[128,1024]{0,1:T(8,128)(2,1)S(1)} %bitcast.93), channel_id=1, source_target_pairs={{2,0},{4,2},{6,4},{3,1},{5,3},{7,5},{10,8},{12,10},{14,12},{11,9},... | collective-permute-start | bytes 786440 | tf_op jit(solution)/shard_map/ppermute | solution.py:13
  20.1 12.0 %copy-start.5 = (bf16[1,128,1024]{2,1,0:T(8,128)(2,1)S(1)}, bf16[1,128,1024]{2,1,0:T(8,128)(2,1)}, u32[]{:S(2)}) copy-start(bf16[1,128,1024]{2,1,0:T(8,128)(2,1)} %param.12) | copy-start | bytes 786436
  26.3 30.9 %collective-permute-start.1 = (bf16[128,2048]{0,1:T(8,128)(2,1)}, bf16[128,2048]{0,1:T(8,128)(2,1)}, u32[]{:S(2)}, u32[]{:S(2)}) collective-permute-start(bf16[128,2048]{0,1:T(8,128)(2,1)} %collective-permute-done), channel_id=1, source_target_pairs={{0,2},{2,4},{4,6},{1,3},{3,5},{5,7},{8,10},{10,12},{12,14},{9,11},... | collective-permute-start | bytes 1572872 | tf_op jit(solution)/shard_map/ppermute | solution.py:13
  35.3 15.7 %collective-permute-start.6 = (bf16[128,1024]{0,1:T(8,128)(2,1)}, bf16[128,1024]{0,1:T(8,128)(2,1)S(1)}, u32[]{:S(2)}, u32[]{:S(2)}) collective-permute-start(bf16[128,1024]{0,1:T(8,128)(2,1)} %collective-permute-done.5), channel_id=1, source_target_pairs={{2,0},{4,2},{6,4},{3,1},{5,3},{7,5},{10,8},{12,10},{14,12},{11,9},... | collective-permute-start | bytes 786440 | tf_op jit(solution)/shard_map/ppermute | solution.py:13
  39.4 20.4 %collective-permute-start.3 = (bf16[128,2048]{0,1:T(8,128)(2,1)}, bf16[128,2048]{0,1:T(8,128)(2,1)}, u32[]{:S(2)}, u32[]{:S(2)}) collective-permute-start(bf16[128,2048]{0,1:T(8,128)(2,1)} %fusion.17), channel_id=1, source_target_pairs={{16,0},{24,8},{17,1},{25,9},{18,2},{26,10},{19,3},{27,11},{20,4},{... | collective-permute-start | bytes 1572872 | tf_op jit(solution)/shard_map/ppermute | solution.py:13
  57.2 14.5 %slice-start = ((s8[8388608]{0:T(1024)(128)(4,1)}), s8[4194304]{0:T(1024)(128)(4,1)S(1)}, s32[]{:S(2)}) async-start(s8[8388608]{0:T(1024)(128)(4,1)} %bitcast.79), calls=%async_computation.2 | async-start | bytes 8388608
  59.8 3.3 %copy-start.2 = (bf16[1,128,1024]{1,2,0:T(8,128)(2,1)S(1)}, bf16[1,128,1024]{1,2,0:T(8,128)(2,1)}, u32[]{:S(2)}) copy-start(bf16[1,128,1024]{1,2,0:T(8,128)(2,1)} %copy-done.1) | copy-start | bytes 786436
  60.0 11.7 %slice-start.1 = ((s8[8388608]{0:T(1024)(128)(4,1)}), s8[4194304]{0:T(1024)(128)(4,1)S(1)}, s32[]{:S(2)}) async-start(s8[8388608]{0:T(1024)(128)(4,1)} %bitcast.79), calls=%async_computation.3 | async-start | bytes 8388608
  61.5 13.7 %collective-permute-start.4 = (bf16[128,2048]{0,1:T(8,128)(2,1)S(1)}, bf16[128,2048]{0,1:T(8,128)(2,1)S(1)}, u32[]{:S(2)}, u32[]{:S(2)}) collective-permute-start(bf16[128,2048]{0,1:T(8,128)(2,1)S(1)} %get-tuple-element.31), channel_id=1, source_target_pairs={{0,1},{1,0},{2,3},{3,2},{4,5},{5,4},{6,7},{7,6},{8,9},{9,8},{10,11... | collective-permute-start | bytes 1572872 | tf_op jit(solution)/shard_map/ppermute | solution.py:63
  63.8 6.0 %collective-permute-start.7 = (f32[8,128]{1,0:T(8,128)S(1)}, f32[8,128]{1,0:T(8,128)S(1)}, u32[]{:S(2)}, u32[]{:S(2)}) collective-permute-start(f32[8,128]{1,0:T(8,128)S(1)} %log_add_fusion), channel_id=1, source_target_pairs={{2,0},{4,2},{6,4},{3,1},{5,3},{7,5},{10,8},{12,10},{14,12},{11,9},... | collective-permute-start | bytes 12296 | tf_op jit(solution)/shard_map/ppermute | solution.py:13
  69.8 5.5 %collective-permute-start.8 = (f32[8,128]{1,0:T(8,128)S(1)}, f32[8,128]{1,0:T(8,128)S(1)}, u32[]{:S(2)}, u32[]{:S(2)}) collective-permute-start(f32[8,128]{1,0:T(8,128)S(1)} %collective-permute-done.7), channel_id=1, source_target_pairs={{2,0},{4,2},{6,4},{3,1},{5,3},{7,5},{10,8},{12,10},{14,12},{11,9},... | collective-permute-start | bytes 12296 | tf_op jit(solution)/shard_map/ppermute | solution.py:13
  76.7 12.4 %collective-permute-start.9 = (bf16[128,1024]{1,0:T(8,128)(2,1)}, bf16[128,1024]{1,0:T(8,128)(2,1)}, u32[]{:S(2)}, u32[]{:S(2)}) collective-permute-start(bf16[128,1024]{1,0:T(8,128)(2,1)} %fusion.13), channel_id=1, source_target_pairs={{2,0},{4,2},{6,4},{3,1},{5,3},{7,5},{10,8},{12,10},{14,12},{11,9},... | collective-permute-start | bytes 786440 | tf_op jit(solution)/shard_map/ppermute | solution.py:13
  80.6 48.2 %all-to-all-start = ((bf16[128,4,1024]{0,2,1:T(8,128)(2,1)}), bf16[128,4,1024]{0,2,1:T(8,128)(2,1)S(1)}, u32[]{:S(2)}, u32[]{:S(2)}) async-start(bf16[128,4,1024]{0,2,1:T(8,128)(2,1)} %bitcast.86), calls=%async_computation | async-start | bytes 2097152 | tf_op jit(solution)/shard_map/all_to_all | solution.py:74
  89.1 27.2 %collective-permute-start.10 = (bf16[128,1024]{1,0:T(8,128)(2,1)}, bf16[128,1024]{1,0:T(8,128)(2,1)}, u32[]{:S(2)}, u32[]{:S(2)}) collective-permute-start(bf16[128,1024]{1,0:T(8,128)(2,1)} %collective-permute-done.9), channel_id=1, source_target_pairs={{2,0},{4,2},{6,4},{3,1},{5,3},{7,5},{10,8},{12,10},{14,12},{11,9},... | collective-permute-start | bytes 786440 | tf_op jit(solution)/shard_map/ppermute | solution.py:13
  121.3 4.6 %copy-start.7 = (bf16[384,8,128]{0,2,1:T(8,128)(2,1)S(1)}, bf16[384,8,128]{0,2,1:T(8,128)(2,1)}, u32[]{:S(2)}) copy-start(bf16[384,8,128]{0,2,1:T(8,128)(2,1)} %copy.130) | copy-start | bytes 2359300
  (7 other events, 16.7 us)
Sparse Core Ops, SparseCore 0:
  19.8 38.5 all-gather.2

commit v2 on v1

v2 whole, which is shorter than its diff:
```python
import jax
import jax.numpy as jnp
from jax import lax
from jax.experimental import pallas as pl
from jax.experimental.pallas import tpu as pltpu
from jax.sharding import PartitionSpec as P

HD = 128
REACH = 2


def passed_along(value, axis, steps):
    count = lax.axis_size(axis)
    leading, last = (max(0, -steps), min(count, count - steps))
    return lax.ppermute(value, axis, [(source, source + steps) for source in range(leading, last)])


def suffix_sum(own, axis):
    count = lax.axis_size(axis)
    total = own.astype(jnp.float32)
    step = 1
    while step < count:
        total = total + passed_along(total.astype(jnp.bfloat16), axis, -step).astype(jnp.float32)
        step *= 2
    return total


def document_of(positions, ends):
    return jnp.sum((positions[:, None] >= ends[None, :]).astype(jnp.int32), axis=-1)


def nt(a, b):
    return lax.dot_general(a, b, (((1,), (1,)), ((), ())), preferred_element_type=jnp.float32)


def tn(a, b):
    return lax.dot_general(a, b, (((0,), (0,)), ((), ())), preferred_element_type=jnp.float32)


def head_columns(head, offset=0):
    return slice(offset + head * HD, offset + (head + 1) * HD)


def stacked(refs, columns):
    return jnp.concatenate([ref[:, columns] for ref in refs], 0)


def delta_row(d_context, context):
    product = d_context.astype(jnp.float32) * context.astype(jnp.float32)
    return jnp.sum(jnp.transpose(product), axis=0, keepdims=True)


def totals_kernel(mask_ref, query_ref, *refs):
    kv_refs, total_ref = refs[:-1], refs[-1]
    allowed = mask_ref[...] > 0.0
    for head in range(query_ref.shape[1] // HD):
        columns = head_columns(head)
        scores = nt(stacked(kv_refs, columns), query_ref[:, columns]) * HD ** (-0.5)
        scores = jnp.where(allowed, scores, -jnp.inf)
        peak = jnp.max(scores, axis=0, keepdims=True)
        total = jnp.sum(jnp.exp(scores - peak), axis=0, keepdims=True)
        total_ref[head : head + 1, :] = peak + jnp.log(total)


def query_kernel(mask_ref, query_ref, dctx_ref, context_ref, total_ref, *refs):
    kv_refs, out_ref = refs[:-1], refs[-1]
    scaling = HD ** (-0.5)
    width = query_ref.shape[1]
    allowed = mask_ref[...] > 0.0
    for head in range(width // HD):
        columns = head_columns(head)
        keys = stacked(kv_refs, columns)
        d_context = dctx_ref[:, columns]
        scores = nt(keys, query_ref[:, columns]) * scaling
        prob = jnp.exp(jnp.where(allowed, scores - total_ref[head : head + 1, :], -jnp.inf))
        d_prob = nt(stacked(kv_refs, head_columns(head, width)), d_context)
        delta = delta_row(d_context, context_ref[:, columns])
        d_score = (prob * (d_prob - delta) * scaling).astype(jnp.bfloat16)
        out_ref[:, columns] = tn(d_score, keys).astype(out_ref.dtype)


def key_kernel(sets, mask_ref, key_ref, value_ref, total_ref, *refs):
    query_refs, dctx_refs = refs[:sets], refs[sets : 2 * sets]
    context_refs = refs[2 * sets : 3 * sets]
    key_out, value_out = refs[3 * sets :]
    scaling = HD ** (-0.5)
    allowed = mask_ref[...] > 0.0
    for head in range(key_ref.shape[1] // HD):
        columns = head_columns(head)
        queries = stacked(query_refs, columns)
        d_context = stacked(dctx_refs, columns)
        scores = nt(key_ref[:, columns], queries) * scaling
        prob = jnp.exp(jnp.where(allowed, scores - total_ref[head : head + 1, :], -jnp.inf))
        d_prob = nt(value_ref[:, columns], d_context)
        delta = jnp.concatenate(
            [delta_row(d[:, columns], c[:, columns]) for d, c in zip(dctx_refs, context_refs)], 1
        )
        d_score = (prob * (d_prob - delta) * scaling).astype(jnp.bfloat16)
        key_out[:, columns] = jnp.dot(
            d_score, queries, preferred_element_type=jnp.float32
        ).astype(key_out.dtype)
        value_out[:, columns] = jnp.dot(
            prob.astype(jnp.bfloat16), d_context, preferred_element_type=jnp.float32
        ).astype(value_out.dtype)


def local_kernel(body, shapes, operands, flops):
    whole = pl.BlockSpec(memory_space=pltpu.VMEM)
    moved = sum(a.size * a.dtype.itemsize for a in (*operands, *shapes))
    return pl.pallas_call(
        body,
        out_shape=shapes,
        in_specs=[whole] * len(operands),
        out_specs=[whole] * len(shapes),
        compiler_params=pltpu.CompilerParams(vmem_limit_bytes=32 * 1024 * 1024),
        cost_estimate=pl.CostEstimate(flops=flops, bytes_accessed=moved, transcendentals=0),
    )(*operands)


def on_device(out_grad, section_out, context, queries, key_heads, values, o_weight, doc_lengths):
    rows, width = (queries.shape[1], queries.shape[2])
    head_count = width // HD
    n_dp, n_tensor = lax.axis_size("dp"), lax.axis_size("tensor")
    dp_at, tensor_at = lax.axis_index("dp"), lax.axis_index("tensor")
    docs = doc_lengths.shape[0]
    ends = jnp.sum(
        jnp.where(jnp.arange(docs)[:, None] >= jnp.arange(docs)[None, :], doc_lengths[None, :], 0),
        axis=1,
    )
    first = dp_at * rows
    window = (REACH + 1) * rows

    kv = jnp.concatenate([key_heads[0], values[0]], 1)
    kv_sets, query_sets = [kv], [queries[0]]
    kv_sets.append(passed_along(kv, "dp", 1))
    query_sets.append(passed_along(queries[0], "dp", -1))
    upper = suffix_sum(section_out[0], "section")
    grad_local = (out_grad.astype(jnp.float32) + 0.25 * upper).astype(jnp.bfloat16)
    context_all = lax.all_gather(context[0], "dp", axis=0, tiled=True)

    grad_local, kv_on, query_on = lax.optimization_barrier(
        (grad_local, kv_sets[-1], query_sets[-1])
    )
    kv_sets[-1], query_sets[-1] = kv_on, query_on
    for step in range(1, REACH):
        kv_sets.append(passed_along(kv_sets[-1], "dp", 1))
        query_sets.append(passed_along(query_sets[-1], "dp", -1))

    local_width = grad_local.shape[1]
    grad_full = jnp.zeros((rows, local_width * n_tensor), jnp.bfloat16)
    d_context = jnp.zeros((rows, width), jnp.float32)
    for step in range(n_tensor):
        part = grad_local
        if step:
            part = lax.ppermute(
                grad_local, "tensor", [(i, (i + step) % n_tensor) for i in range(n_tensor)]
            )
        start = lax.rem(tensor_at + n_tensor - step, n_tensor) * local_width
        grad_full = lax.dynamic_update_slice_in_dim(grad_full, part, start, 1)
        weight = lax.dynamic_slice_in_dim(o_weight[0], start, local_width, 0)
        d_context = d_context + jnp.dot(part, weight, preferred_element_type=jnp.float32)
    d_context = d_context.astype(jnp.bfloat16)
    dctx_sets = [d_context]
    for step in range(REACH):
        dctx_sets.append(passed_along(dctx_sets[-1], "dp", -1))
    grad_blocks = lax.all_to_all(grad_full, "dp", split_axis=1, concat_axis=0, tiled=True)

    own_place = first + jnp.arange(rows, dtype=jnp.int32)
    own_docs = document_of(own_place, ends)
    window_place = first - REACH * rows + jnp.arange(window, dtype=jnp.int32)
    window_docs = document_of(window_place, ends)
    allowed = (
        (window_docs[:, None] == own_docs[None, :])
        & (window_place[:, None] <= own_place[None, :])
        & (window_place[:, None] >= 0)
    ).astype(jnp.float32)
    work = 2 * window * rows * width
    kv_win = kv_sets[::-1]
    (total,) = local_kernel(
        totals_kernel,
        [jax.ShapeDtypeStruct((head_count, rows), jnp.float32)],
        (allowed, queries[0], *kv_win),
        work,
    )
    total_sets = [total]
    for step in range(REACH):
        total_sets.append(passed_along(total_sets[-1], "dp", -1))
    flat = jax.ShapeDtypeStruct((rows, width), jnp.bfloat16)
    (query_grad,) = local_kernel(
        query_kernel,
        [flat],
        (allowed, queries[0], d_context, context[0], total, *kv_win),
        3 * work,
    )

    set_place = first + jnp.arange(window, dtype=jnp.int32)
    set_docs = document_of(set_place, ends)
    allowed_back = (
        (own_docs[:, None] == set_docs[None, :])
        & (own_place[:, None] <= set_place[None, :])
        & (set_place[None, :] < n_dp * rows)
    ).astype(jnp.float32)
    context_sets = [context[0]]
    for step in range(1, REACH + 1):
        at = jnp.minimum(dp_at + step, n_dp - 1) * rows
        context_sets.append(lax.dynamic_slice_in_dim(context_all, at, rows, 0))
    key_grad, value_grad = local_kernel(
        lambda *refs: key_kernel(REACH + 1, *refs),
        [flat, flat],
        (
            allowed_back,
            key_heads[0],
            values[0],
            jnp.concatenate(total_sets, 1),
            *query_sets,
            *dctx_sets,
            *context_sets,
        ),
        4 * work,
    )
    weight_grad = lax.dot_general(
        grad_blocks, context_all, (((0,), (0,)), ((), ())), preferred_element_type=jnp.float32
    )
    return query_grad[None], key_grad[None], value_grad[None], weight_grad[None]


def solution(mesh):
    placed = (
        P("dp", "tensor"),
        P("section", "dp", "tensor"),
        P("section", "dp", "tensor"),
        P("section", "dp", "tensor"),
        P("section", "dp", "tensor"),
        P("section", "dp", "tensor"),
        P("section", None, "tensor"),
        P(),
    )
    return jax.shard_map(
        on_device,
        mesh=mesh,
        in_specs=placed,
        out_specs=(
            P("section", "dp", "tensor"),
            P("section", "dp", "tensor"),
            P("section", "dp", "tensor"),
            P("section", "dp", "tensor"),
        ),
        check_vma=False,
    )
```

time: 140 us -> 132 us (0.943); the launches traced: 139 us -> 130 us
  local copies, waits for them, and re-layouts: 19.1 us -> 7.18 us
  waiting for transfers between devices: 43.9 us -> 51.8 us
  Pallas kernels: 0 us -> 7.74 us
  other arithmetic: 10.9 us -> 3.39 us
  matrix products: 16 us -> 10.4 us
    dot_general x5 -> x0, matrix products: 10.5 us -> none  [the longest x1 3.71 us: on_device(): jnp.einsum('hij,ihd->jhd', d_score_back, query_set, preferred_element_typ...]
    pallas_call x0 -> x3, Pallas kernels: none -> 7.74 us  [local_kernel(): pl.pallas_call(body, out_shape=shapes, in_specs=[whole] * len(operands),...]
    ppermute x1, waiting for transfers between devices: 0.01 us -> 7.11 us  [on_device(): lax.ppermute(grad_local, 'tensor', [(i, (i + step) % n_tensor) for i in r...]
    unnamed x50 -> x14, local copies, waits for them, and re-layouts: 11.4 us -> 4.35 us
    dot_general x2, matrix products: 2.19 us -> 5.91 us  [on_device(): jnp.dot(part, weight, preferred_element_type=jnp.float32)]
    ppermute x10, starting transfers between devices: 26.4 us -> 23.7 us  [passed_along(): lax.ppermute(value, axis, [(source, source + steps) for source in range(l...]
    reduce_sum x3 -> x0, other arithmetic: 2.7 us -> none  [the longest x1 1.32 us: on_device(): jnp.sum(dctx_b.astype(jnp.float32) * context[0].reshape(three).astype(jnp...]
    concatenate x2 -> x0, local copies, waits for them, and re-layouts: 2.64 us -> none  [on_device(): query_set = jnp.concatenate(query_flat, 0).reshape(window, head_count, HD)]
  transfers between devices with their start and end apart: 13 -> 13, of which waited for: 6 -> 6; matrix products, arithmetic and copies ran while one was open for 28% -> 10% of each run, Pallas kernels for 0% -> 6%
where the time goes in v2:
time: 132 us; the launch traced here: 130 us
  waiting for transfers between devices  51.8 us (39%)
  starting transfers between devices  35.1 us (27%)
  between operations  14.3 us (11%)
  matrix products  10.4 us (8%)
  Pallas kernels  7.74 us (6%)
  local copies, waits for them, and re-layouts  7.18 us (5%)
  other arithmetic  3.39 us (3%)
    ppermute x10, waiting for transfers between devices, passed_along(): lax.ppermute(value, axis, [(source, source + steps) for source in range(l...  44.7 us
    ppermute x10, starting transfers between devices, passed_along(): lax.ppermute(value, axis, [(source, source + steps) for source in range(l...  23.7 us
    all_to_all x1, starting transfers between devices, on_device(): lax.all_to_all(grad_full, 'dp', split_axis=1, concat_axis=0, tiled=True)  9.72 us
    pallas_call x3, Pallas kernels, local_kernel(): pl.pallas_call(body, out_shape=shapes, in_specs=[whole] * len(operands),...  7.74 us
    ppermute x1, waiting for transfers between devices, on_device(): lax.ppermute(grad_local, 'tensor', [(i, (i + step) % n_tensor) for i in r...  7.11 us
    dot_general x2, matrix products, on_device(): jnp.dot(part, weight, preferred_element_type=jnp.float32)  5.91 us
    dot_general x1, matrix products, on_device(): lax.dot_general(grad_blocks, context_all, (((0,), (0,)), ((), ())), prefe...  4.53 us
    unnamed x14, local copies, waits for them, and re-layouts  4.35 us
  transfers between devices with their start and end apart: 13, of which 6 were waited for; matrix products, arithmetic and copies ran while one was open for 10% of the time, Pallas kernels for 6%

profile of v2, /device:TPU:12, one launch (start us, length us, event | category | flops | bytes accessed | tf_op | source)
XLA Modules:
  0.0 130.0 jit_solution(1638694406096692569)
XLA Ops:
  8.5 1.9 %collective-permute-start = (bf16[128,2048]{0,1:T(8,128)(2,1)S(1)}, bf16[128,2048]{0,1:T(8,128)(2,1)S(1)}, u32[]{:S(2)}, u32[]{:S(2)}) collective-permute-start(bf16[128,2048]{0,1:T(8,128)(2,1)S(1)} %bitcast.45), channel_id=1, source_target_pairs={{8,0},{16,8},{24,16},{9,1},{17,9},{25,17},{10,2},{18,10},{26,18},{... | collective-permute-start | bytes 1572872 | tf_op jit(solution)/shard_map/ppermute | solution.py:15
  10.5 6.7 %collective-permute-done = bf16[128,2048]{0,1:T(8,128)(2,1)S(1)} collective-permute-done((bf16[128,2048]{0,1:T(8,128)(2,1)S(1)}, bf16[128,2048]{0,1:T(8,128)(2,1)S(1)}, u32[]{:S(2)}, u32[]{:S(2)}) %collective-permute-start) | collective-permute-done | bytes 524320 | tf_op jit(solution)/shard_map/ppermute | solution.py:15
  17.3 2.1 %collective-permute-start.1 = (bf16[128,2048]{0,1:T(8,128)(2,1)S(1)}, bf16[128,2048]{0,1:T(8,128)(2,1)}, u32[]{:S(2)}, u32[]{:S(2)}) collective-permute-start(bf16[128,2048]{0,1:T(8,128)(2,1)S(1)} %fusion.13), channel_id=1, source_target_pairs={{16,0},{24,8},{17,1},{25,9},{18,2},{26,10},{19,3},{27,11},{20,4},{... | collective-permute-start | bytes 1572872 | tf_op jit(solution)/shard_map/ppermute | solution.py:15
  19.4 2.4 %collective-permute-start.3 = (bf16[128,1024]{1,0:T(8,128)(2,1)}, bf16[128,1024]{1,0:T(8,128)(2,1)S(1)}, u32[]{:S(2)}, u32[]{:S(2)}) collective-permute-start(bf16[128,1024]{1,0:T(8,128)(2,1)} %bitcast.37), channel_id=1, source_target_pairs={{2,0},{4,2},{6,4},{3,1},{5,3},{7,5},{10,8},{12,10},{14,12},{11,9},... | collective-permute-start | bytes 786440 | tf_op jit(solution)/shard_map/ppermute | solution.py:15
  22.9 3.5 %collective-permute-start.2 = (bf16[128,2048]{1,0:T(8,128)(2,1)S(1)}, bf16[128,2048]{1,0:T(8,128)(2,1)S(1)}, u32[]{:S(2)}, u32[]{:S(2)}) collective-permute-start(bf16[128,2048]{1,0:T(8,128)(2,1)S(1)} %pad_maximum_fusion.refs_2_), channel_id=1, source_target_pairs={{0,2},{2,4},{4,6},{1,3},{3,5},{5,7},{8,10},{10,12},{12,14},{9,11},... | collective-permute-start | bytes 1572872 | tf_op jit(solution)/shard_map/ppermute | solution.py:15
  26.4 2.0 %copy.15 = bf16[128,2048]{0,1:T(8,128)(2,1)} copy(bf16[128,2048]{1,0:T(8,128)(2,1)} %param.8) | data formatting | bytes 1048576 | tf_op args[0]
  28.9 1.5 %add_convert_fusion = bf16[128,2048]{0,1:T(8,128)(2,1)S(1)} fusion(bf16[128,2048]{0,1:T(8,128)(2,1)} %collective-permute-done.1, bf16[128,2048]{0,1:T(8,128)(2,1)} %copy.15, bf16[128,2048]{0,1:T(8,128)(2,1)S(1)} %collective-permute-done, bf16[1,128,2048]{1,2,0:T(8,128)(2,1)S(1)} %copy.16), kind=kLoop, calls=%fused_computation.10 | loop fusion | flops 2359296 | bytes 2621440 | tf_op jit(solution)/shard_map/convert_element_type | solution.py:138
  30.4 16.5 %collective-permute-done.2.refs_1_ = bf16[128,2048]{1,0:T(8,128)(2,1)S(1)} collective-permute-done((bf16[128,2048]{1,0:T(8,128)(2,1)S(1)}, bf16[128,2048]{1,0:T(8,128)(2,1)S(1)}, u32[]{:S(2)}, u32[]{:S(2)}) %collective-permute-start.2) | collective-permute-done | bytes 524320 | tf_op jit(solution)/shard_map/ppermute | solution.py:15
  46.9 1.6 %collective-permute-start.4 = (bf16[128,2048]{0,1:T(8,128)(2,1)S(1)}, bf16[128,2048]{0,1:T(8,128)(2,1)S(1)}, u32[]{:S(2)}, u32[]{:S(2)}) collective-permute-start(bf16[128,2048]{0,1:T(8,128)(2,1)S(1)} %add_convert_fusion), channel_id=1, source_target_pairs={{0,1},{1,0},{2,3},{3,2},{4,5},{5,4},{6,7},{7,6},{8,9},{9,8},{10,11... | collective-permute-start | bytes 1572872 | tf_op jit(solution)/shard_map/ppermute | solution.py:155
  49.0 7.1 %collective-permute-done.4 = bf16[128,2048]{0,1:T(8,128)(2,1)S(1)} collective-permute-done((bf16[128,2048]{0,1:T(8,128)(2,1)S(1)}, bf16[128,2048]{0,1:T(8,128)(2,1)S(1)}, u32[]{:S(2)}, u32[]{:S(2)}) %collective-permute-start.4) | collective-permute-done | bytes 524320 | tf_op jit(solution)/shard_map/ppermute | solution.py:155
  57.2 9.7 %all-to-all-start = ((bf16[128,4,1024]{0,2,1:T(8,128)(2,1)}), bf16[128,4,1024]{0,2,1:T(8,128)(2,1)}, u32[]{:S(2)}, u32[]{:S(2)}) async-start(bf16[128,4,1024]{0,2,1:T(8,128)(2,1)} %bitcast.46), calls=%async_computation | async-start | bytes 2097152 | tf_op jit(solution)/shard_map/all_to_all | solution.py:166
  67.1 3.5 %collective-permute-start.5 = (bf16[128,2048]{1,0:T(8,128)(2,1)S(1)}, bf16[128,2048]{1,0:T(8,128)(2,1)S(1)}, u32[]{:S(2)}, u32[]{:S(2)}) collective-permute-start(bf16[128,2048]{1,0:T(8,128)(2,1)S(1)} %collective-permute-done.2.refs_1_), channel_id=1, source_target_pairs={{0,2},{2,4},{4,6},{1,3},{3,5},{5,7},{8,10},{10,12},{12,14},{9,11},... | collective-permute-start | bytes 1572872 | tf_op jit(solution)/shard_map/ppermute | solution.py:15
  70.6 2.9 %fusion = f32[128,1024]{1,0:T(8,128)S(1)} fusion(bf16[128,2048]{0,1:T(8,128)(2,1)S(1)} %collective-permute-done.4, bf16[1,4096,1024]{2,1,0:T(8,128)(2,1)} %param.14, s32[]{:T(128)S(6)} %select_n.20), kind=kOutput, calls=%fused_computation | convolution fusion | flops 536870912 | bytes 5242884 | tf_op jit(solution)/shard_map/dot_general | solution.py:161
  73.6 3.0 %fusion.9.dctx_ref.refs_7_ = bf16[128,1024]{1,0:T(8,128)(2,1)S(1)} fusion(f32[128,1024]{1,0:T(8,128)S(1)} %fusion, bf16[128,2048]{0,1:T(8,128)(2,1)S(1)} %add_convert_fusion, bf16[1,4096,1024]{2,1,0:T(8,128)(2,1)} %param.14, s32[]{:T(128)S(6)} %select_n.19), kind=kOutput, calls=%fused_computation.8 | convolution fusion | flops 537133056 | bytes 5505028 | tf_op jit(solution)/shard_map/dot_general | solution.py:161
  76.6 2.6 %collective-permute-start.9 = (bf16[128,1024]{1,0:T(8,128)(2,1)S(1)}, bf16[128,1024]{1,0:T(8,128)(2,1)}, u32[]{:S(2)}, u32[]{:S(2)}) collective-permute-start(bf16[128,1024]{1,0:T(8,128)(2,1)S(1)} %fusion.9.dctx_ref.refs_7_), channel_id=1, source_target_pairs={{2,0},{4,2},{6,4},{3,1},{5,3},{7,5},{10,8},{12,10},{14,12},{11,9},... | collective-permute-start | bytes 786440 | tf_op jit(solution)/shard_map/ppermute | solution.py:15
  79.5 1.9 %collective-permute-start.8 = (bf16[128,1024]{1,0:T(8,128)(2,1)S(1)}, bf16[128,1024]{1,0:T(8,128)(2,1)}, u32[]{:S(2)}, u32[]{:S(2)}) collective-permute-start(bf16[128,1024]{1,0:T(8,128)(2,1)S(1)} %collective-permute-done.3.refs_5_), channel_id=1, source_target_pairs={{2,0},{4,2},{6,4},{3,1},{5,3},{7,5},{10,8},{12,10},{14,12},{11,9},... | collective-permute-start | bytes 786440 | tf_op jit(solution)/shard_map/ppermute | solution.py:15
  81.4 18.0 %collective-permute-done.5.refs_0_ = bf16[128,2048]{1,0:T(8,128)(2,1)S(1)} collective-permute-done((bf16[128,2048]{1,0:T(8,128)(2,1)S(1)}, bf16[128,2048]{1,0:T(8,128)(2,1)S(1)}, u32[]{:S(2)}, u32[]{:S(2)}) %collective-permute-start.5) | collective-permute-done | bytes 524320 | tf_op jit(solution)/shard_map/ppermute | solution.py:15
  100.1 1.9 %collective-permute-start.6 = (f32[8,128]{1,0:T(8,128)S(1)}, f32[8,128]{1,0:T(8,128)S(1)}, u32[]{:S(2)}, u32[]{:S(2)}) collective-permute-start(f32[8,128]{1,0:T(8,128)S(1)} %shard_map.111.total_ref), channel_id=1, source_target_pairs={{2,0},{4,2},{6,4},{3,1},{5,3},{7,5},{10,8},{12,10},{14,12},{11,9},... | collective-permute-start | bytes 12296 | tf_op jit(solution)/shard_map/ppermute | solution.py:15
  102.0 1.9 %collective-permute-start.10 = (bf16[128,1024]{1,0:T(8,128)(2,1)}, bf16[128,1024]{1,0:T(8,128)(2,1)}, u32[]{:S(2)}, u32[]{:S(2)}) collective-permute-start(bf16[128,1024]{1,0:T(8,128)(2,1)} %collective-permute-done.9.refs_8_), channel_id=1, source_target_pairs={{2,0},{4,2},{6,4},{3,1},{5,3},{7,5},{10,8},{12,10},{14,12},{11,9},... | collective-permute-start | bytes 786440 | tf_op jit(solution)/shard_map/ppermute | solution.py:15
  104.0 3.0 %shard_map.112 = bf16[128,1024]{1,0:T(8,128)(2,1)} custom-call(f32[384,128]{1,0:T(8,128)S(1)} %and_convert_fusion.1.mask_ref, bf16[128,1024]{1,0:T(8,128)(2,1)S(1)} %bitcast.39, bf16[128,1024]{1,0:T(8,128)(2,1)S(1)} %fusion.9.dctx_ref.refs_7_, bf16[128,1024]{1,0:T(8,128)(2,1)S(1)} %bitcast.35, f32[8,128]{1,0:T(8,128)S(1)} %shard_map.111.total_ref, ...), custom_call_target="tpu_custom_call" | custom-call | flops 301989888 | bytes 2822144 | tf_op jit(solution)/shard_map/pallas_call | solution.py:110
  107.0 1.9 %collective-permute-start.7 = (f32[8,128]{1,0:T(8,128)S(1)}, f32[8,128]{1,0:T(8,128)S(1)}, u32[]{:S(2)}, u32[]{:S(2)}) collective-permute-start(f32[8,128]{1,0:T(8,128)S(1)} %collective-permute-done.6), channel_id=1, source_target_pairs={{2,0},{4,2},{6,4},{3,1},{5,3},{7,5},{10,8},{12,10},{14,12},{11,9},... | collective-permute-start | bytes 12296 | tf_op jit(solution)/shard_map/ppermute | solution.py:15
  110.0 3.0 %collective-permute-done.7 = f32[8,128]{1,0:T(8,128)S(1)} collective-permute-done((f32[8,128]{1,0:T(8,128)S(1)}, f32[8,128]{1,0:T(8,128)S(1)}, u32[]{:S(2)}, u32[]{:S(2)}) %collective-permute-start.7) | collective-permute-done | bytes 4128 | tf_op jit(solution)/shard_map/ppermute | solution.py:15
  113.1 4.1 %shard_map.113 = (bf16[128,1024]{1,0:T(8,128)(2,1)}, bf16[128,1024]{1,0:T(8,128)(2,1)}) custom-call(f32[128,384]{1,0:T(8,128)S(1)} %and_convert_fusion.refs_0_, bf16[128,1024]{1,0:T(8,128)(2,1)S(1)} %bitcast.44, bf16[128,1024]{1,0:T(8,128)(2,1)S(1)} %bitcast.42, f32[8,384]{1,0:T(8,128)S(1)} %pad_maximum_fusion.1.refs_3_, bf16[128,1024]{1,0:T(8,128)(2,1)S(1)} %bitcast.40, ...), custom_call_target="tpu_custom_call" | custom-call | flops 402653184 | bytes 3616768 | tf_op jit(solution)/shard_map/pallas_call | solution.py:110
  118.6 4.5 %convolution_bitcast_fusion = f32[1,1024,1024]{2,1,0:T(8,128)} fusion(bf16[512,1024]{1,0:T(8,128)(2,1)S(1)} %bitcast.47, bf16[1,512,1024]{2,1,0:T(8,128)(2,1)} %all-gather.3.cloned.1.call-done), kind=kOutput, calls=%fused_computation.6 | convolution fusion | flops 1073741824 | bytes 6291456 | tf_op jit(solution)/shard_map/dot_general | solution.py:221
  (42 shorter events, 8.2 us)
Async XLA Ops:
  7.2 41.4 %copy-start.5 = (s32[4]{0:T(128)S(1)}, s32[4]{0:T(128)}, u32[]{:S(2)}) copy-start(s32[4]{0:T(128)} %param.15) | copy-start | bytes 52
  7.2 101.7 %all-gather.3.cloned.1.call-start = ((), (), s32[]{:S(2)}) async-start(), calls=%async_computation.1 | async-start | bytes 1310720 | tf_op jit(solution)/shard_map/all_gather | solution.py:139
  8.5 8.6 %collective-permute-start = (bf16[128,2048]{0,1:T(8,128)(2,1)S(1)}, bf16[128,2048]{0,1:T(8,128)(2,1)S(1)}, u32[]{:S(2)}, u32[]{:S(2)}) collective-permute-start(bf16[128,2048]{0,1:T(8,128)(2,1)S(1)} %bitcast.45), channel_id=1, source_target_pairs={{8,0},{16,8},{24,16},{9,1},{17,9},{25,17},{10,2},{18,10},{26,18},{... | collective-permute-start | bytes 1572872 | tf_op jit(solution)/shard_map/ppermute | solution.py:15
  17.3 11.6 %collective-permute-start.1 = (bf16[128,2048]{0,1:T(8,128)(2,1)S(1)}, bf16[128,2048]{0,1:T(8,128)(2,1)}, u32[]{:S(2)}, u32[]{:S(2)}) collective-permute-start(bf16[128,2048]{0,1:T(8,128)(2,1)S(1)} %fusion.13), channel_id=1, source_target_pairs={{16,0},{24,8},{17,1},{25,9},{18,2},{26,10},{19,3},{27,11},{20,4},{... | collective-permute-start | bytes 1572872 | tf_op jit(solution)/shard_map/ppermute | solution.py:15
  19.4 11.0 %collective-permute-start.3 = (bf16[128,1024]{1,0:T(8,128)(2,1)}, bf16[128,1024]{1,0:T(8,128)(2,1)S(1)}, u32[]{:S(2)}, u32[]{:S(2)}) collective-permute-start(bf16[128,1024]{1,0:T(8,128)(2,1)} %bitcast.37), channel_id=1, source_target_pairs={{2,0},{4,2},{6,4},{3,1},{5,3},{7,5},{10,8},{12,10},{14,12},{11,9},... | collective-permute-start | bytes 786440 | tf_op jit(solution)/shard_map/ppermute | solution.py:15
  22.9 24.1 %collective-permute-start.2 = (bf16[128,2048]{1,0:T(8,128)(2,1)S(1)}, bf16[128,2048]{1,0:T(8,128)(2,1)S(1)}, u32[]{:S(2)}, u32[]{:S(2)}) collective-permute-start(bf16[128,2048]{1,0:T(8,128)(2,1)S(1)} %pad_maximum_fusion.refs_2_), channel_id=1, source_target_pairs={{0,2},{2,4},{4,6},{1,3},{3,5},{5,7},{8,10},{10,12},{12,14},{9,11},... | collective-permute-start | bytes 1572872 | tf_op jit(solution)/shard_map/ppermute | solution.py:15
  46.9 9.2 %collective-permute-start.4 = (bf16[128,2048]{0,1:T(8,128)(2,1)S(1)}, bf16[128,2048]{0,1:T(8,128)(2,1)S(1)}, u32[]{:S(2)}, u32[]{:S(2)}) collective-permute-start(bf16[128,2048]{0,1:T(8,128)(2,1)S(1)} %add_convert_fusion), channel_id=1, source_target_pairs={{0,1},{1,0},{2,3},{3,2},{4,5},{5,4},{6,7},{7,6},{8,9},{9,8},{10,11... | collective-permute-start | bytes 1572872 | tf_op jit(solution)/shard_map/ppermute | solution.py:155
  56.2 1.0 copy-start.4
  57.2 60.0 %all-to-all-start = ((bf16[128,4,1024]{0,2,1:T(8,128)(2,1)}), bf16[128,4,1024]{0,2,1:T(8,128)(2,1)}, u32[]{:S(2)}, u32[]{:S(2)}) async-start(bf16[128,4,1024]{0,2,1:T(8,128)(2,1)} %bitcast.46), calls=%async_computation | async-start | bytes 2097152 | tf_op jit(solution)/shard_map/all_to_all | solution.py:166
  67.1 32.3 %copy-start.1 = (bf16[1,128,1024]{2,1,0:T(8,128)(2,1)S(1)}, bf16[1,128,1024]{2,1,0:T(8,128)(2,1)}, u32[]{:S(2)}) copy-start(bf16[1,128,1024]{2,1,0:T(8,128)(2,1)} %param.11) | copy-start | bytes 786436
  67.1 32.3 %collective-permute-start.5 = (bf16[128,2048]{1,0:T(8,128)(2,1)S(1)}, bf16[128,2048]{1,0:T(8,128)(2,1)S(1)}, u32[]{:S(2)}, u32[]{:S(2)}) collective-permute-start(bf16[128,2048]{1,0:T(8,128)(2,1)S(1)} %collective-permute-done.2.refs_1_), channel_id=1, source_target_pairs={{0,2},{2,4},{4,6},{1,3},{3,5},{5,7},{8,10},{10,12},{12,14},{9,11},... | collective-permute-start | bytes 1572872 | tf_op jit(solution)/shard_map/ppermute | solution.py:15
  73.6 30.4 %copy-start = (bf16[1,128,1024]{2,1,0:T(8,128)(2,1)S(1)}, bf16[1,128,1024]{2,1,0:T(8,128)(2,1)}, u32[]{:S(2)}) copy-start(bf16[1,128,1024]{2,1,0:T(8,128)(2,1)} %param.10) | copy-start | bytes 786436
  76.6 36.5 %copy-start.2 = (bf16[1,128,1024]{2,1,0:T(8,128)(2,1)S(1)}, bf16[1,128,1024]{2,1,0:T(8,128)(2,1)}, u32[]{:S(2)}) copy-start(bf16[1,128,1024]{2,1,0:T(8,128)(2,1)} %param.13) | copy-start | bytes 786436
  76.6 36.5 %copy-start.3 = (bf16[1,128,1024]{2,1,0:T(8,128)(2,1)S(1)}, bf16[1,128,1024]{2,1,0:T(8,128)(2,1)}, u32[]{:S(2)}) copy-start(bf16[1,128,1024]{2,1,0:T(8,128)(2,1)} %param.12) | copy-start | bytes 786436
  76.6 25.4 %collective-permute-start.9 = (bf16[128,1024]{1,0:T(8,128)(2,1)S(1)}, bf16[128,1024]{1,0:T(8,128)(2,1)}, u32[]{:S(2)}, u32[]{:S(2)}) collective-permute-start(bf16[128,1024]{1,0:T(8,128)(2,1)S(1)} %fusion.9.dctx_ref.refs_7_), channel_id=1, source_target_pairs={{2,0},{4,2},{6,4},{3,1},{5,3},{7,5},{10,8},{12,10},{14,12},{11,9},... | collective-permute-start | bytes 786440 | tf_op jit(solution)/shard_map/ppermute | solution.py:15
  79.5 33.6 %collective-permute-start.8 = (bf16[128,1024]{1,0:T(8,128)(2,1)S(1)}, bf16[128,1024]{1,0:T(8,128)(2,1)}, u32[]{:S(2)}, u32[]{:S(2)}) collective-permute-start(bf16[128,1024]{1,0:T(8,128)(2,1)S(1)} %collective-permute-done.3.refs_5_), channel_id=1, source_target_pairs={{2,0},{4,2},{6,4},{3,1},{5,3},{7,5},{10,8},{12,10},{14,12},{11,9},... | collective-permute-start | bytes 786440 | tf_op jit(solution)/shard_map/ppermute | solution.py:15
  100.1 6.9 %collective-permute-start.6 = (f32[8,128]{1,0:T(8,128)S(1)}, f32[8,128]{1,0:T(8,128)S(1)}, u32[]{:S(2)}, u32[]{:S(2)}) collective-permute-start(f32[8,128]{1,0:T(8,128)S(1)} %shard_map.111.total_ref), channel_id=1, source_target_pairs={{2,0},{4,2},{6,4},{3,1},{5,3},{7,5},{10,8},{12,10},{14,12},{11,9},... | collective-permute-start | bytes 12296 | tf_op jit(solution)/shard_map/ppermute | solution.py:15
  102.0 11.0 %collective-permute-start.10 = (bf16[128,1024]{1,0:T(8,128)(2,1)}, bf16[128,1024]{1,0:T(8,128)(2,1)}, u32[]{:S(2)}, u32[]{:S(2)}) collective-permute-start(bf16[128,1024]{1,0:T(8,128)(2,1)} %collective-permute-done.9.refs_8_), channel_id=1, source_target_pairs={{2,0},{4,2},{6,4},{3,1},{5,3},{7,5},{10,8},{12,10},{14,12},{11,9},... | collective-permute-start | bytes 786440 | tf_op jit(solution)/shard_map/ppermute | solution.py:15
  107.0 6.1 %collective-permute-start.7 = (f32[8,128]{1,0:T(8,128)S(1)}, f32[8,128]{1,0:T(8,128)S(1)}, u32[]{:S(2)}, u32[]{:S(2)}) collective-permute-start(f32[8,128]{1,0:T(8,128)S(1)} %collective-permute-done.6), channel_id=1, source_target_pairs={{2,0},{4,2},{6,4},{3,1},{5,3},{7,5},{10,8},{12,10},{14,12},{11,9},... | collective-permute-start | bytes 12296 | tf_op jit(solution)/shard_map/ppermute | solution.py:15
Sparse Core Ops, SparseCore 0:
  19.6 37.1 all-gather.2

commit v3 on v2

--- a/solution.py
+++ b/solution.py
@@ -50,7 +50,8 @@
     return jnp.sum(jnp.transpose(product), axis=0, keepdims=True)
 
 
-def totals_kernel(mask_ref, query_ref, *refs):
+def totals_kernel(after_ref, mask_ref, query_ref, *refs):
+    del after_ref
     kv_refs, total_ref = refs[:-1], refs[-1]
     allowed = mask_ref[...] > 0.0
     for head in range(query_ref.shape[1] // HD):
@@ -131,20 +132,14 @@
     window = (REACH + 1) * rows
 
     kv = jnp.concatenate([key_heads[0], values[0]], 1)
+    own_out, kv, context_own = lax.optimization_barrier((section_out[0], kv, context[0]))
     kv_sets, query_sets = [kv], [queries[0]]
-    kv_sets.append(passed_along(kv, "dp", 1))
-    query_sets.append(passed_along(queries[0], "dp", -1))
-    upper = suffix_sum(section_out[0], "section")
+    for step in range(1, REACH + 1):
+        kv_sets.append(passed_along(kv, "dp", step))
+        query_sets.append(passed_along(queries[0], "dp", -step))
+    upper = suffix_sum(own_out, "section")
     grad_local = (out_grad.astype(jnp.float32) + 0.25 * upper).astype(jnp.bfloat16)
-    context_all = lax.all_gather(context[0], "dp", axis=0, tiled=True)
-
-    grad_local, kv_on, query_on = lax.optimization_barrier(
-        (grad_local, kv_sets[-1], query_sets[-1])
-    )
-    kv_sets[-1], query_sets[-1] = kv_on, query_on
-    for step in range(1, REACH):
-        kv_sets.append(passed_along(kv_sets[-1], "dp", 1))
-        query_sets.append(passed_along(query_sets[-1], "dp", -1))
+    context_all = lax.all_gather(context_own, "dp", axis=0, tiled=True)
 
     local_width = grad_local.shape[1]
     grad_full = jnp.zeros((rows, local_width * n_tensor), jnp.bfloat16)
@@ -179,12 +174,12 @@
     (total,) = local_kernel(
         totals_kernel,
         [jax.ShapeDtypeStruct((head_count, rows), jnp.float32)],
-        (allowed, queries[0], *kv_win),
+        (d_context, allowed, queries[0], *kv_win),
         work,
     )
     total_sets = [total]
-    for step in range(REACH):
-        total_sets.append(passed_along(total_sets[-1], "dp", -1))
+    for step in range(1, REACH + 1):
+        total_sets.append(passed_along(total, "dp", -step))
     flat = jax.ShapeDtypeStruct((rows, width), jnp.bfloat16)
     (query_grad,) = local_kernel(
         query_kernel,

time: 132 us -> 123 us (0.932); the launches traced: 130 us -> 123 us
  waiting for transfers between devices: 51.8 us -> 44.5 us
  starting transfers between devices: 35.1 us -> 31.7 us
  other arithmetic: 3.39 us -> 5.95 us
    ppermute x10, waiting for transfers between devices: 44.7 us -> 32.2 us  [passed_along(): lax.ppermute(value, axis, [(source, source + steps) for source in range(l...]
    ppermute x1, waiting for transfers between devices: 7.11 us -> 12.3 us  [on_device(): lax.ppermute(grad_local, 'tensor', [(i, (i + step) % n_tensor) for i in r...]
    all_to_all x1, starting transfers between devices: 9.72 us -> 7.29 us  [on_device(): lax.all_to_all(grad_full, 'dp', split_axis=1, concat_axis=0, tiled=True)]
    dynamic_update_slice x0 -> x1, other arithmetic: none -> 2.14 us  [on_device(): grad_full = lax.dynamic_update_slice_in_dim(grad_full, part, start, 1)]
    convert_element_type x1 -> x0, other arithmetic: 1.54 us -> none  [on_device(): (out_grad.astype(jnp.float32) + 0.25 * upper).astype(jnp.bfloat16)]
  transfers between devices with their start and end apart: 13 -> 13, of which waited for: 6 -> 5; matrix products, arithmetic and copies ran while one was open for 10% -> 12% of each run, Pallas kernels for 6% -> 6%
where the time goes in v3:
time: 123 us
  waiting for transfers between devices  44.5 us (36%)
  starting transfers between devices  31.7 us (26%)
  between operations  14.3 us (12%)
  matrix products  10.7 us (9%)
  local copies, waits for them, and re-layouts  7.93 us (6%)
  Pallas kernels  7.74 us (6%)
  other arithmetic  5.95 us (5%)
    ppermute x10, waiting for transfers between devices, passed_along(): lax.ppermute(value, axis, [(source, source + steps) for source in range(l...  32.2 us
    ppermute x10, starting transfers between devices, passed_along(): lax.ppermute(value, axis, [(source, source + steps) for source in range(l...  22.9 us
    ppermute x1, waiting for transfers between devices, on_device(): lax.ppermute(grad_local, 'tensor', [(i, (i + step) % n_tensor) for i in r...  12.3 us
    pallas_call x3, Pallas kernels, local_kernel(): pl.pallas_call(body, out_shape=shapes, in_specs=[whole] * len(operands),...  7.74 us
    all_to_all x1, starting transfers between devices, on_device(): lax.all_to_all(grad_full, 'dp', split_axis=1, concat_axis=0, tiled=True)  7.29 us
    dot_general x2, matrix products, on_device(): jnp.dot(part, weight, preferred_element_type=jnp.float32)  6.13 us
    dot_general x1, matrix products, on_device(): lax.dot_general(grad_blocks, context_all, (((0,), (0,)), ((), ())), prefe...  4.53 us
    unnamed x14, local copies, waits for them, and re-layouts  3.45 us
  transfers between devices with their start and end apart: 13, of which 5 were waited for; matrix products, arithmetic and copies ran while one was open for 12% of the time, Pallas kernels for 6%

profile of v3, /device:TPU:12, one launch (start us, length us, event | category | flops | bytes accessed | tf_op | source)
XLA Modules:
  0.0 122.8 jit_solution(12270603956096016490)
XLA Ops:
  7.2 1.3 %copy.16 = bf16[1,128,2048]{1,2,0:T(8,128)(2,1)S(1)} copy(bf16[1,128,2048]{2,1,0:T(8,128)(2,1)} %param.9) | data formatting | bytes 1048576 | tf_op args[1]
  9.6 1.9 %collective-permute-start = (bf16[128,2048]{0,1:T(8,128)(2,1)S(1)}, bf16[128,2048]{0,1:T(8,128)(2,1)S(1)}, u32[]{:S(2)}, u32[]{:S(2)}) collective-permute-start(bf16[128,2048]{0,1:T(8,128)(2,1)S(1)} %bitcast.39), channel_id=1, source_target_pairs={{8,0},{16,8},{24,16},{9,1},{17,9},{25,17},{10,2},{18,10},{26,18},{... | collective-permute-start | bytes 1572872 | tf_op jit(solution)/shard_map/ppermute | solution.py:15
  11.5 6.7 %collective-permute-done = bf16[128,2048]{0,1:T(8,128)(2,1)S(1)} collective-permute-done((bf16[128,2048]{0,1:T(8,128)(2,1)S(1)}, bf16[128,2048]{0,1:T(8,128)(2,1)S(1)}, u32[]{:S(2)}, u32[]{:S(2)}) %collective-permute-start) | collective-permute-done | bytes 524320 | tf_op jit(solution)/shard_map/ppermute | solution.py:15
  19.2 2.1 %collective-permute-start.1 = (bf16[128,2048]{0,1:T(8,128)(2,1)}, bf16[128,2048]{0,1:T(8,128)(2,1)}, u32[]{:S(2)}, u32[]{:S(2)}) collective-permute-start(bf16[128,2048]{0,1:T(8,128)(2,1)} %fusion.12), channel_id=1, source_target_pairs={{16,0},{24,8},{17,1},{25,9},{18,2},{26,10},{19,3},{27,11},{20,4},{... | collective-permute-start | bytes 1572872 | tf_op jit(solution)/shard_map/ppermute | solution.py:15
  21.3 4.5 %collective-permute-start.3 = (bf16[128,2048]{1,0:T(8,128)(2,1)S(1)}, bf16[128,2048]{1,0:T(8,128)(2,1)S(1)}, u32[]{:S(2)}, u32[]{:S(2)}) collective-permute-start(bf16[128,2048]{1,0:T(8,128)(2,1)S(1)} %pad_maximum_fusion.refs_2_), channel_id=1, source_target_pairs={{0,4},{2,6},{1,5},{3,7},{8,12},{10,14},{9,13},{11,15},{16,20},{18,... | collective-permute-start | bytes 1572872 | tf_op jit(solution)/shard_map/ppermute | solution.py:15
  25.8 1.9 %collective-permute-start.4 = (bf16[128,2048]{1,0:T(8,128)(2,1)S(1)}, bf16[128,2048]{1,0:T(8,128)(2,1)S(1)}, u32[]{:S(2)}, u32[]{:S(2)}) collective-permute-start(bf16[128,2048]{1,0:T(8,128)(2,1)S(1)} %pad_maximum_fusion.refs_2_), channel_id=1, source_target_pairs={{0,2},{2,4},{4,6},{1,3},{3,5},{5,7},{8,10},{10,12},{12,14},{9,11},... | collective-permute-start | bytes 1572872 | tf_op jit(solution)/shard_map/ppermute | solution.py:15
  27.7 4.0 %collective-permute-start.7 = (bf16[128,1024]{1,0:T(8,128)(2,1)}, bf16[128,1024]{1,0:T(8,128)(2,1)S(1)}, u32[]{:S(2)}, u32[]{:S(2)}) collective-permute-start(bf16[128,1024]{1,0:T(8,128)(2,1)} %bitcast.27), channel_id=1, source_target_pairs={{2,0},{4,2},{6,4},{3,1},{5,3},{7,5},{10,8},{12,10},{14,12},{11,9},... | collective-permute-start | bytes 786440 | tf_op jit(solution)/shard_map/ppermute | solution.py:15
  33.0 1.3 %copy.15 = bf16[128,2048]{0,1:T(8,128)(2,1)S(1)} copy(bf16[128,2048]{1,0:T(8,128)(2,1)} %param.8) | data formatting | bytes 1048576 | tf_op args[0]
  35.5 2.1 %constant_dynamic-update-slice_fusion.1 = (bf16[128,4096]{0,1:T(8,128)(2,1)}, bf16[128,2048]{0,1:T(8,128)(2,1)S(1)}) fusion(bf16[128,4096]{0,1:T(8,128)(2,1)} %broadcast_in_dim.27, s32[]{:T(128)S(6)} %select_n.19, bf16[128,2048]{0,1:T(8,128)(2,1)} %collective-permute-done.1, bf16[128,2048]{0,1:T(8,128)(2,1)S(1)} %collective-permute-done, ...), kind=kLoop, calls=%fused_computation.24 | loop fusion | flops 2359296 | bytes 3145732 | tf_op jit(solution)/shard_map/dynamic_update_slice | solution.py:154
  38.4 1.5 %collective-permute-start.2 = (bf16[128,2048]{0,1:T(8,128)(2,1)S(1)}, bf16[128,2048]{0,1:T(8,128)(2,1)S(1)}, u32[]{:S(2)}, u32[]{:S(2)}) collective-permute-start(bf16[128,2048]{0,1:T(8,128)(2,1)S(1)} %get-tuple-element.17), channel_id=1, source_target_pairs={{0,1},{1,0},{2,3},{3,2},{4,5},{5,4},{6,7},{7,6},{8,9},{9,8},{10,11... | collective-permute-start | bytes 1572872 | tf_op jit(solution)/shard_map/ppermute | solution.py:150
  40.1 12.3 %collective-permute-done.2 = bf16[128,2048]{0,1:T(8,128)(2,1)S(1)} collective-permute-done((bf16[128,2048]{0,1:T(8,128)(2,1)S(1)}, bf16[128,2048]{0,1:T(8,128)(2,1)S(1)}, u32[]{:S(2)}, u32[]{:S(2)}) %collective-permute-start.2) | collective-permute-done | bytes 524320 | tf_op jit(solution)/shard_map/ppermute | solution.py:150
  53.2 7.3 %all-to-all-start = ((bf16[128,4,1024]{0,2,1:T(8,128)(2,1)}), bf16[128,4,1024]{0,2,1:T(8,128)(2,1)}, u32[]{:S(2)}, u32[]{:S(2)}) async-start(bf16[128,4,1024]{0,2,1:T(8,128)(2,1)} %bitcast.10), calls=%async_computation | async-start | bytes 2097152 | tf_op jit(solution)/shard_map/all_to_all | solution.py:161
  60.9 3.2 %fusion.2 = f32[128,1024]{1,0:T(8,128)S(1)} fusion(bf16[128,2048]{0,1:T(8,128)(2,1)} %copy-done.4, bf16[1,4096,1024]{2,1,0:T(8,128)(2,1)} %param.14, s32[]{:T(128)S(6)} %select_n.19), kind=kOutput, calls=%fused_computation.2 | convolution fusion | flops 536870912 | bytes 5242884 | tf_op jit(solution)/shard_map/dot_general | solution.py:156
  64.0 3.0 %fusion.9.after_ref.dctx_ref.refs_7_ = bf16[128,1024]{1,0:T(8,128)(2,1)S(1)} fusion(f32[128,1024]{1,0:T(8,128)S(1)} %fusion.2, bf16[128,2048]{0,1:T(8,128)(2,1)S(1)} %collective-permute-done.2, bf16[1,4096,1024]{2,1,0:T(8,128)(2,1)} %param.14, s32[]{:T(128)S(6)} %select_n.20), kind=kOutput, calls=%fused_computation.8 | convolution fusion | flops 537133056 | bytes 5505028 | tf_op jit(solution)/shard_map/dot_general | solution.py:156
  67.0 2.1 %collective-permute-start.9 = (bf16[128,1024]{1,0:T(8,128)(2,1)S(1)}, bf16[128,1024]{1,0:T(8,128)(2,1)}, u32[]{:S(2)}, u32[]{:S(2)}) collective-permute-start(bf16[128,1024]{1,0:T(8,128)(2,1)S(1)} %fusion.9.after_ref.dctx_ref.refs_7_), channel_id=1, source_target_pairs={{2,0},{4,2},{6,4},{3,1},{5,3},{7,5},{10,8},{12,10},{14,12},{11,9},... | collective-permute-start | bytes 786440 | tf_op jit(solution)/shard_map/ppermute | solution.py:15
  70.4 18.1 %collective-permute-done.4.refs_1_ = bf16[128,2048]{1,0:T(8,128)(2,1)S(1)} collective-permute-done((bf16[128,2048]{1,0:T(8,128)(2,1)S(1)}, bf16[128,2048]{1,0:T(8,128)(2,1)S(1)}, u32[]{:S(2)}, u32[]{:S(2)}) %collective-permute-start.4) | collective-permute-done | bytes 524320 | tf_op jit(solution)/shard_map/ppermute | solution.py:15
  90.4 1.9 %collective-permute-start.5 = (f32[8,128]{1,0:T(8,128)S(1)}, f32[8,128]{1,0:T(8,128)S(1)}, u32[]{:S(2)}, u32[]{:S(2)}) collective-permute-start(f32[8,128]{1,0:T(8,128)S(1)} %shard_map.111.total_ref), channel_id=1, source_target_pairs={{2,0},{4,2},{6,4},{3,1},{5,3},{7,5},{10,8},{12,10},{14,12},{11,9},... | collective-permute-start | bytes 12296 | tf_op jit(solution)/shard_map/ppermute | solution.py:15
  92.4 3.0 %collective-permute-done.9.refs_8_ = bf16[128,1024]{1,0:T(8,128)(2,1)} collective-permute-done((bf16[128,1024]{1,0:T(8,128)(2,1)S(1)}, bf16[128,1024]{1,0:T(8,128)(2,1)}, u32[]{:S(2)}, u32[]{:S(2)}) %collective-permute-start.9) | collective-permute-done | bytes 262176 | tf_op jit(solution)/shard_map/ppermute | solution.py:15
  95.4 1.9 %collective-permute-start.10 = (bf16[128,1024]{1,0:T(8,128)(2,1)}, bf16[128,1024]{1,0:T(8,128)(2,1)}, u32[]{:S(2)}, u32[]{:S(2)}) collective-permute-start(bf16[128,1024]{1,0:T(8,128)(2,1)} %collective-permute-done.9.refs_8_), channel_id=1, source_target_pairs={{2,0},{4,2},{6,4},{3,1},{5,3},{7,5},{10,8},{12,10},{14,12},{11,9},... | collective-permute-start | bytes 786440 | tf_op jit(solution)/shard_map/ppermute | solution.py:15
  97.3 3.0 %shard_map.112 = bf16[128,1024]{1,0:T(8,128)(2,1)} custom-call(f32[384,128]{1,0:T(8,128)S(1)} %and_convert_fusion.1.mask_ref, bf16[128,1024]{1,0:T(8,128)(2,1)S(1)} %bitcast.30, bf16[128,1024]{1,0:T(8,128)(2,1)S(1)} %fusion.9.after_ref.dctx_ref.refs_7_, bf16[128,1024]{1,0:T(8,128)(2,1)S(1)} %bitcast.33, f32[8,128]{1,0:T(8,128)S(1)} %shard_map.111.total_ref, ...), custom_call_target="tpu_custom_call" | custom-call | flops 301989888 | bytes 2822144 | tf_op jit(solution)/shard_map/pallas_call | solution.py:111
  101.5 4.4 %collective-permute-done.10.refs_9_ = bf16[128,1024]{1,0:T(8,128)(2,1)} collective-permute-done((bf16[128,1024]{1,0:T(8,128)(2,1)}, bf16[128,1024]{1,0:T(8,128)(2,1)}, u32[]{:S(2)}, u32[]{:S(2)}) %collective-permute-start.10) | collective-permute-done | bytes 262176 | tf_op jit(solution)/shard_map/ppermute | solution.py:15
  105.9 4.1 %shard_map.113 = (bf16[128,1024]{1,0:T(8,128)(2,1)}, bf16[128,1024]{1,0:T(8,128)(2,1)}) custom-call(f32[128,384]{1,0:T(8,128)S(1)} %and_convert_fusion.refs_0_, bf16[128,1024]{1,0:T(8,128)(2,1)S(1)} %bitcast.38, bf16[128,1024]{1,0:T(8,128)(2,1)S(1)} %bitcast.36, f32[8,384]{1,0:T(8,128)S(1)} %pad_maximum_fusion.1.refs_3_, bf16[128,1024]{1,0:T(8,128)(2,1)S(1)} %bitcast.31, ...), custom_call_target="tpu_custom_call" | custom-call | flops 402653184 | bytes 3616768 | tf_op jit(solution)/shard_map/pallas_call | solution.py:111
  109.9 1.5 %copy.17 = bf16[4,128,1024]{2,1,0:T(8,128)(2,1)S(1)} copy(bf16[4,128,1024]{1,2,0:T(8,128)(2,1)} %bitcast.11) | data formatting | bytes 2097152 | tf_op jit(solution)/shard_map/all_to_all | solution.py:161
  111.4 4.5 %convolution_bitcast_fusion = f32[1,1024,1024]{2,1,0:T(8,128)} fusion(bf16[512,1024]{1,0:T(8,128)(2,1)S(1)} %bitcast.42, bf16[512,1024]{1,0:T(8,128)(2,1)} %all-gather.2.cloned.1.call-done), kind=kOutput, calls=%fused_computation.6 | convolution fusion | flops 1073741824 | bytes 6291456 | tf_op jit(solution)/shard_map/dot_general | solution.py:216
  (41 shorter events, 11.0 us)
Async XLA Ops:
  7.2 93.2 %all-gather.2.cloned.1.call-start = ((), (), s32[]{:S(2)}) async-start(), calls=%async_computation.1 | async-start | bytes 1310720 | tf_op jit(solution)/shard_map/all_gather | solution.py:142
  8.5 31.4 %copy-start.5 = (s32[4]{0:T(128)S(1)}, s32[4]{0:T(128)}, u32[]{:S(2)}) copy-start(s32[4]{0:T(128)} %param.15) | copy-start | bytes 52
  9.6 8.6 %collective-permute-start = (bf16[128,2048]{0,1:T(8,128)(2,1)S(1)}, bf16[128,2048]{0,1:T(8,128)(2,1)S(1)}, u32[]{:S(2)}, u32[]{:S(2)}) collective-permute-start(bf16[128,2048]{0,1:T(8,128)(2,1)S(1)} %bitcast.39), channel_id=1, source_target_pairs={{8,0},{16,8},{24,16},{9,1},{17,9},{25,17},{10,2},{18,10},{26,18},{... | collective-permute-start | bytes 1572872 | tf_op jit(solution)/shard_map/ppermute | solution.py:15
  19.2 15.2 %collective-permute-start.1 = (bf16[128,2048]{0,1:T(8,128)(2,1)}, bf16[128,2048]{0,1:T(8,128)(2,1)}, u32[]{:S(2)}, u32[]{:S(2)}) collective-permute-start(bf16[128,2048]{0,1:T(8,128)(2,1)} %fusion.12), channel_id=1, source_target_pairs={{16,0},{24,8},{17,1},{25,9},{18,2},{26,10},{19,3},{27,11},{20,4},{... | collective-permute-start | bytes 1572872 | tf_op jit(solution)/shard_map/ppermute | solution.py:15
  21.3 49.1 %collective-permute-start.3 = (bf16[128,2048]{1,0:T(8,128)(2,1)S(1)}, bf16[128,2048]{1,0:T(8,128)(2,1)S(1)}, u32[]{:S(2)}, u32[]{:S(2)}) collective-permute-start(bf16[128,2048]{1,0:T(8,128)(2,1)S(1)} %pad_maximum_fusion.refs_2_), channel_id=1, source_target_pairs={{0,4},{2,6},{1,5},{3,7},{8,12},{10,14},{9,13},{11,15},{16,20},{18,... | collective-permute-start | bytes 1572872 | tf_op jit(solution)/shard_map/ppermute | solution.py:15
  25.8 62.7 %collective-permute-start.4 = (bf16[128,2048]{1,0:T(8,128)(2,1)S(1)}, bf16[128,2048]{1,0:T(8,128)(2,1)S(1)}, u32[]{:S(2)}, u32[]{:S(2)}) collective-permute-start(bf16[128,2048]{1,0:T(8,128)(2,1)S(1)} %pad_maximum_fusion.refs_2_), channel_id=1, source_target_pairs={{0,2},{2,4},{4,6},{1,3},{3,5},{5,7},{8,10},{10,12},{12,14},{9,11},... | collective-permute-start | bytes 1572872 | tf_op jit(solution)/shard_map/ppermute | solution.py:15
  27.7 73.7 %collective-permute-start.7 = (bf16[128,1024]{1,0:T(8,128)(2,1)}, bf16[128,1024]{1,0:T(8,128)(2,1)S(1)}, u32[]{:S(2)}, u32[]{:S(2)}) collective-permute-start(bf16[128,1024]{1,0:T(8,128)(2,1)} %bitcast.27), channel_id=1, source_target_pairs={{2,0},{4,2},{6,4},{3,1},{5,3},{7,5},{10,8},{12,10},{14,12},{11,9},... | collective-permute-start | bytes 786440 | tf_op jit(solution)/shard_map/ppermute | solution.py:15
  31.7 69.8 %collective-permute-start.8 = (bf16[128,1024]{1,0:T(8,128)(2,1)}, bf16[128,1024]{1,0:T(8,128)(2,1)}, u32[]{:S(2)}, u32[]{:S(2)}) collective-permute-start(bf16[128,1024]{1,0:T(8,128)(2,1)} %bitcast.28), channel_id=1, source_target_pairs={{4,0},{6,2},{5,1},{7,3},{12,8},{14,10},{13,9},{15,11},{20,16},{22,... | collective-permute-start | bytes 786440 | tf_op jit(solution)/shard_map/ppermute | solution.py:15
  37.6 0.8 copy-start.4
  38.4 14.0 %collective-permute-start.2 = (bf16[128,2048]{0,1:T(8,128)(2,1)S(1)}, bf16[128,2048]{0,1:T(8,128)(2,1)S(1)}, u32[]{:S(2)}, u32[]{:S(2)}) collective-permute-start(bf16[128,2048]{0,1:T(8,128)(2,1)S(1)} %get-tuple-element.17), channel_id=1, source_target_pairs={{0,1},{1,0},{2,3},{3,2},{4,5},{5,4},{6,7},{7,6},{8,9},{9,8},{10,11... | collective-permute-start | bytes 1572872 | tf_op jit(solution)/shard_map/ppermute | solution.py:150
  53.2 56.7 %all-to-all-start = ((bf16[128,4,1024]{0,2,1:T(8,128)(2,1)}), bf16[128,4,1024]{0,2,1:T(8,128)(2,1)}, u32[]{:S(2)}, u32[]{:S(2)}) async-start(bf16[128,4,1024]{0,2,1:T(8,128)(2,1)} %bitcast.10), calls=%async_computation | async-start | bytes 2097152 | tf_op jit(solution)/shard_map/all_to_all | solution.py:161
  60.9 27.6 %copy-start = (bf16[1,128,1024]{2,1,0:T(8,128)(2,1)S(1)}, bf16[1,128,1024]{2,1,0:T(8,128)(2,1)}, u32[]{:S(2)}) copy-start(bf16[1,128,1024]{2,1,0:T(8,128)(2,1)} %param.11) | copy-start | bytes 786436
  64.0 33.3 %copy-start.1 = (bf16[1,128,1024]{2,1,0:T(8,128)(2,1)S(1)}, bf16[1,128,1024]{2,1,0:T(8,128)(2,1)}, u32[]{:S(2)}) copy-start(bf16[1,128,1024]{2,1,0:T(8,128)(2,1)} %param.10) | copy-start | bytes 786436
  67.0 38.8 %copy-start.2 = (bf16[1,128,1024]{2,1,0:T(8,128)(2,1)S(1)}, bf16[1,128,1024]{2,1,0:T(8,128)(2,1)}, u32[]{:S(2)}) copy-start(bf16[1,128,1024]{2,1,0:T(8,128)(2,1)} %param.13) | copy-start | bytes 786436
  67.0 38.8 %copy-start.3 = (bf16[1,128,1024]{2,1,0:T(8,128)(2,1)S(1)}, bf16[1,128,1024]{2,1,0:T(8,128)(2,1)}, u32[]{:S(2)}) copy-start(bf16[1,128,1024]{2,1,0:T(8,128)(2,1)} %param.12) | copy-start | bytes 786436
  67.0 28.4 %collective-permute-start.9 = (bf16[128,1024]{1,0:T(8,128)(2,1)S(1)}, bf16[128,1024]{1,0:T(8,128)(2,1)}, u32[]{:S(2)}, u32[]{:S(2)}) collective-permute-start(bf16[128,1024]{1,0:T(8,128)(2,1)S(1)} %fusion.9.after_ref.dctx_ref.refs_7_), channel_id=1, source_target_pairs={{2,0},{4,2},{6,4},{3,1},{5,3},{7,5},{10,8},{12,10},{14,12},{11,9},... | collective-permute-start | bytes 786440 | tf_op jit(solution)/shard_map/ppermute | solution.py:15
  89.1 12.3 %collective-permute-start.6 = (f32[8,128]{1,0:T(8,128)S(1)}, f32[8,128]{1,0:T(8,128)S(1)}, u32[]{:S(2)}, u32[]{:S(2)}) collective-permute-start(f32[8,128]{1,0:T(8,128)S(1)} %shard_map.111.total_ref), channel_id=1, source_target_pairs={{4,0},{6,2},{5,1},{7,3},{12,8},{14,10},{13,9},{15,11},{20,16},{22,... | collective-permute-start | bytes 12296 | tf_op jit(solution)/shard_map/ppermute | solution.py:15
  90.4 11.0 %collective-permute-start.5 = (f32[8,128]{1,0:T(8,128)S(1)}, f32[8,128]{1,0:T(8,128)S(1)}, u32[]{:S(2)}, u32[]{:S(2)}) collective-permute-start(f32[8,128]{1,0:T(8,128)S(1)} %shard_map.111.total_ref), channel_id=1, source_target_pairs={{2,0},{4,2},{6,4},{3,1},{5,3},{7,5},{10,8},{12,10},{14,12},{11,9},... | collective-permute-start | bytes 12296 | tf_op jit(solution)/shard_map/ppermute | solution.py:15
  95.4 10.4 %collective-permute-start.10 = (bf16[128,1024]{1,0:T(8,128)(2,1)}, bf16[128,1024]{1,0:T(8,128)(2,1)}, u32[]{:S(2)}, u32[]{:S(2)}) collective-permute-start(bf16[128,1024]{1,0:T(8,128)(2,1)} %collective-permute-done.9.refs_8_), channel_id=1, source_target_pairs={{2,0},{4,2},{6,4},{3,1},{5,3},{7,5},{10,8},{12,10},{14,12},{11,9},... | collective-permute-start | bytes 786440 | tf_op jit(solution)/shard_map/ppermute | solution.py:15
Sparse Core Ops, SparseCore 0:
  33.1 40.2 all-gather.1

commit v4 on v3

--- a/solution.py
+++ b/solution.py
@@ -158,7 +158,14 @@
     dctx_sets = [d_context]
     for step in range(REACH):
         dctx_sets.append(passed_along(dctx_sets[-1], "dp", -1))
-    grad_blocks = lax.all_to_all(grad_full, "dp", split_axis=1, concat_axis=0, tiled=True)
+    block = grad_full.shape[1] // n_dp
+    share = block // n_tensor
+    grad_share = lax.dynamic_index_in_dim(
+        grad_full.reshape(rows, n_dp, n_tensor, share), tensor_at, 2, keepdims=False
+    )
+    grad_share = lax.all_to_all(
+        grad_share.reshape(rows, n_dp * share), "dp", split_axis=1, concat_axis=0, tiled=True
+    )
 
     own_place = first + jnp.arange(rows, dtype=jnp.int32)
     own_docs = document_of(own_place, ends)
@@ -213,6 +220,15 @@
         ),
         4 * work,
     )
+    grad_blocks = jnp.zeros((n_dp * rows, block), jnp.bfloat16)
+    for step in range(n_tensor):
+        part = grad_share
+        if step:
+            part = lax.ppermute(
+                grad_share, "tensor", [(i, (i + step) % n_tensor) for i in range(n_tensor)]
+            )
+        start = lax.rem(tensor_at + n_tensor - step, n_tensor) * share
+        grad_blocks = lax.dynamic_update_slice_in_dim(grad_blocks, part, start, 1)
     weight_grad = lax.dot_general(
         grad_blocks, context_all, (((0,), (0,)), ((), ())), preferred_element_type=jnp.float32
     )

time: 123 us -> 129 us (1.049); the launches traced: 123 us -> 126 us
  waiting for transfers between devices: 44.5 us -> 49.2 us
  starting transfers between devices: 31.7 us -> 33.4 us
    all_to_all x1, waiting for transfers between devices: 0.01 us -> 26.1 us  [on_device(): lax.all_to_all(grad_share.reshape(rows, n_dp * share), 'dp', split_axis=1...]
    ppermute x10, waiting for transfers between devices: 32.2 us -> 10.9 us  [passed_along(): lax.ppermute(value, axis, [(source, source + steps) for source in range(l...]
    ppermute x10, starting transfers between devices: 22.9 us -> 26.1 us  [passed_along(): lax.ppermute(value, axis, [(source, source + steps) for source in range(l...]
    all_to_all x1, starting transfers between devices: 7.29 us -> 4.13 us  [on_device(): lax.all_to_all(grad_share.reshape(rows, n_dp * share), 'dp', split_axis=1...]
    dynamic_update_slice x0 -> x2, local copies, waits for them, and re-layouts: none -> 2.22 us  [on_device(): grad_blocks = lax.dynamic_update_slice_in_dim(grad_blocks, part, start, 1)]
    ppermute x0 -> x1, starting transfers between devices: none -> 1.49 us  [on_device(): lax.ppermute(grad_share, 'tensor', [(i, (i + step) % n_tensor) for i in r...]
    all_to_all x1 -> x0, local copies, waits for them, and re-layouts: 1.48 us -> none  [on_device(): lax.all_to_all(grad_full, 'dp', split_axis=1, concat_axis=0, tiled=True)]
    unnamed x14 -> x18, local copies, waits for them, and re-layouts: 3.45 us -> 2.66 us
  transfers between devices with their start and end apart: 13 -> 14, of which waited for: 5 -> 5; matrix products, arithmetic and copies ran while one was open for 12% -> 11% of each run, Pallas kernels for 6% -> 6%
where the time goes in v4:
time: 129 us; the launch traced here: 126 us
  waiting for transfers between devices  49.2 us (38%)
  starting transfers between devices  33.4 us (26%)
  between operations  14.5 us (11%)
  matrix products  9.41 us (7%)
  Pallas kernels  7.77 us (6%)
  local copies, waits for them, and re-layouts  7.44 us (6%)
  other arithmetic  4.7 us (4%)
    ppermute x10, starting transfers between devices, passed_along(): lax.ppermute(value, axis, [(source, source + steps) for source in range(l...  26.1 us
    all_to_all x1, waiting for transfers between devices, on_device(): lax.all_to_all(grad_share.reshape(rows, n_dp * share), 'dp', split_axis=1...  26.1 us
    ppermute x1, waiting for transfers between devices, on_device(): lax.ppermute(grad_local, 'tensor', [(i, (i + step) % n_tensor) for i in r...  12.2 us
    ppermute x10, waiting for transfers between devices, passed_along(): lax.ppermute(value, axis, [(source, source + steps) for source in range(l...  10.9 us
    pallas_call x3, Pallas kernels, local_kernel(): pl.pallas_call(body, out_shape=shapes, in_specs=[whole] * len(operands),...  7.77 us
    dot_general x2, matrix products, on_device(): jnp.dot(part, weight, preferred_element_type=jnp.float32)  6.1 us
    all_to_all x1, starting transfers between devices, on_device(): lax.all_to_all(grad_share.reshape(rows, n_dp * share), 'dp', split_axis=1...  4.13 us
    dot_general x1, matrix products, on_device(): lax.dot_general(grad_blocks, context_all, (((0,), (0,)), ((), ())), prefe...  3.31 us
  transfers between devices with their start and end apart: 14, of which 5 were waited for; matrix products, arithmetic and copies ran while one was open for 11% of the time, Pallas kernels for 6%

profile of v4, /device:TPU:12, one launch (start us, length us, event | category | flops | bytes accessed | tf_op | source)
XLA Modules:
  0.0 126.3 jit_solution(7273600588759639361)
XLA Ops:
  7.2 1.3 %copy.16 = bf16[1,128,2048]{1,2,0:T(8,128)(2,1)S(1)} copy(bf16[1,128,2048]{2,1,0:T(8,128)(2,1)} %param.9) | data formatting | bytes 1048576 | tf_op args[1]
  9.6 1.9 %collective-permute-start = (bf16[128,2048]{0,1:T(8,128)(2,1)S(1)}, bf16[128,2048]{0,1:T(8,128)(2,1)S(1)}, u32[]{:S(2)}, u32[]{:S(2)}) collective-permute-start(bf16[128,2048]{0,1:T(8,128)(2,1)S(1)} %bitcast.41), channel_id=1, source_target_pairs={{8,0},{16,8},{24,16},{9,1},{17,9},{25,17},{10,2},{18,10},{26,18},{... | collective-permute-start | bytes 1572872 | tf_op jit(solution)/shard_map/ppermute | solution.py:15
  11.5 6.7 %collective-permute-done = bf16[128,2048]{0,1:T(8,128)(2,1)S(1)} collective-permute-done((bf16[128,2048]{0,1:T(8,128)(2,1)S(1)}, bf16[128,2048]{0,1:T(8,128)(2,1)S(1)}, u32[]{:S(2)}, u32[]{:S(2)}) %collective-permute-start) | collective-permute-done | bytes 524320 | tf_op jit(solution)/shard_map/ppermute | solution.py:15
  19.2 2.1 %collective-permute-start.1 = (bf16[128,2048]{0,1:T(8,128)(2,1)}, bf16[128,2048]{0,1:T(8,128)(2,1)}, u32[]{:S(2)}, u32[]{:S(2)}) collective-permute-start(bf16[128,2048]{0,1:T(8,128)(2,1)} %fusion.12), channel_id=1, source_target_pairs={{16,0},{24,8},{17,1},{25,9},{18,2},{26,10},{19,3},{27,11},{20,4},{... | collective-permute-start | bytes 1572872 | tf_op jit(solution)/shard_map/ppermute | solution.py:15
  21.3 4.5 %collective-permute-start.3 = (bf16[128,2048]{1,0:T(8,128)(2,1)S(1)}, bf16[128,2048]{1,0:T(8,128)(2,1)S(1)}, u32[]{:S(2)}, u32[]{:S(2)}) collective-permute-start(bf16[128,2048]{1,0:T(8,128)(2,1)S(1)} %pad_maximum_fusion.refs_2_), channel_id=1, source_target_pairs={{0,4},{2,6},{1,5},{3,7},{8,12},{10,14},{9,13},{11,15},{16,20},{18,... | collective-permute-start | bytes 1572872 | tf_op jit(solution)/shard_map/ppermute | solution.py:15
  25.8 1.9 %collective-permute-start.4 = (bf16[128,2048]{1,0:T(8,128)(2,1)S(1)}, bf16[128,2048]{1,0:T(8,128)(2,1)S(1)}, u32[]{:S(2)}, u32[]{:S(2)}) collective-permute-start(bf16[128,2048]{1,0:T(8,128)(2,1)S(1)} %pad_maximum_fusion.refs_2_), channel_id=1, source_target_pairs={{0,2},{2,4},{4,6},{1,3},{3,5},{5,7},{8,10},{10,12},{12,14},{9,11},... | collective-permute-start | bytes 1572872 | tf_op jit(solution)/shard_map/ppermute | solution.py:15
  27.7 4.0 %collective-permute-start.7 = (bf16[128,1024]{1,0:T(8,128)(2,1)}, bf16[128,1024]{1,0:T(8,128)(2,1)S(1)}, u32[]{:S(2)}, u32[]{:S(2)}) collective-permute-start(bf16[128,1024]{1,0:T(8,128)(2,1)} %bitcast.29), channel_id=1, source_target_pairs={{2,0},{4,2},{6,4},{3,1},{5,3},{7,5},{10,8},{12,10},{14,12},{11,9},... | collective-permute-start | bytes 786440 | tf_op jit(solution)/shard_map/ppermute | solution.py:15
  31.7 1.3 %copy.15 = bf16[128,2048]{0,1:T(8,128)(2,1)S(1)} copy(bf16[128,2048]{1,0:T(8,128)(2,1)} %param.8) | data formatting | bytes 1048576 | tf_op args[0]
  33.2 1.4 %constant_dynamic-update-slice_fusion.3 = (bf16[128,4096]{0,1:T(8,128)(2,1)S(1)}, bf16[128,2048]{0,1:T(8,128)(2,1)S(1)}) fusion(bf16[128,4096]{0,1:T(8,128)(2,1)S(1)} %broadcast_in_dim.30, s32[]{:T(128)S(6)} %select_n.29, bf16[128,2048]{0,1:T(8,128)(2,1)} %collective-permute-done.1, bf16[128,2048]{0,1:T(8,128)(2,1)S(1)} %collective-permute-done, ...), kind=kLoop, calls=%fused_computation.22 | loop fusion | flops 2359296 | bytes 3145732 | tf_op jit(solution)/shard_map/dynamic_update_slice | solution.py:154
  34.6 1.6 %collective-permute-start.2 = (bf16[128,2048]{0,1:T(8,128)(2,1)S(1)}, bf16[128,2048]{0,1:T(8,128)(2,1)S(1)}, u32[]{:S(2)}, u32[]{:S(2)}) collective-permute-start(bf16[128,2048]{0,1:T(8,128)(2,1)S(1)} %get-tuple-element.17), channel_id=1, source_target_pairs={{0,1},{1,0},{2,3},{3,2},{4,5},{5,4},{6,7},{7,6},{8,9},{9,8},{10,11... | collective-permute-start | bytes 1572872 | tf_op jit(solution)/shard_map/ppermute | solution.py:150
  36.5 12.2 %collective-permute-done.2 = bf16[128,2048]{0,1:T(8,128)(2,1)S(1)} collective-permute-done((bf16[128,2048]{0,1:T(8,128)(2,1)S(1)}, bf16[128,2048]{0,1:T(8,128)(2,1)S(1)}, u32[]{:S(2)}, u32[]{:S(2)}) %collective-permute-start.2) | collective-permute-done | bytes 524320 | tf_op jit(solution)/shard_map/ppermute | solution.py:150
  49.9 4.1 %all-to-all-start = ((bf16[128,4,512]{2,0,1:T(8,128)(2,1)}), bf16[128,4,512]{2,0,1:T(8,128)(2,1)}, u32[]{:S(2)}, u32[]{:S(2)}) async-start(bf16[128,4,512]{2,0,1:T(8,128)(2,1)} %bitcast.11), calls=%async_computation | async-start | bytes 1048576 | tf_op jit(solution)/shard_map/all_to_all | solution.py:166
  54.2 3.1 %fusion.2 = f32[128,1024]{1,0:T(8,128)S(1)} fusion(bf16[128,2048]{0,1:T(8,128)(2,1)} %copy-done.4, bf16[1,4096,1024]{2,1,0:T(8,128)(2,1)} %param.14, s32[]{:T(128)S(6)} %select_n.29), kind=kOutput, calls=%fused_computation.2 | convolution fusion | flops 536870912 | bytes 5242884 | tf_op jit(solution)/shard_map/dot_general | solution.py:156
  57.4 3.0 %fusion.9.after_ref.dctx_ref.refs_7_ = bf16[128,1024]{1,0:T(8,128)(2,1)S(1)} fusion(f32[128,1024]{1,0:T(8,128)S(1)} %fusion.2, bf16[128,2048]{0,1:T(8,128)(2,1)S(1)} %collective-permute-done.2, bf16[1,4096,1024]{2,1,0:T(8,128)(2,1)} %param.14, s32[]{:T(128)S(6)} %select_n.30), kind=kOutput, calls=%fused_computation.8 | convolution fusion | flops 537133056 | bytes 5505028 | tf_op jit(solution)/shard_map/dot_general | solution.py:156
  60.4 2.1 %collective-permute-start.9 = (bf16[128,1024]{1,0:T(8,128)(2,1)S(1)}, bf16[128,1024]{1,0:T(8,128)(2,1)}, u32[]{:S(2)}, u32[]{:S(2)}) collective-permute-start(bf16[128,1024]{1,0:T(8,128)(2,1)S(1)} %fusion.9.after_ref.dctx_ref.refs_7_), channel_id=1, source_target_pairs={{2,0},{4,2},{6,4},{3,1},{5,3},{7,5},{10,8},{12,10},{14,12},{11,9},... | collective-permute-start | bytes 786440 | tf_op jit(solution)/shard_map/ppermute | solution.py:15
  62.5 26.1 %all-to-all-done = bf16[128,4,512]{2,0,1:T(8,128)(2,1)} async-done(((bf16[128,4,512]{2,0,1:T(8,128)(2,1)}), bf16[128,4,512]{2,0,1:T(8,128)(2,1)}, u32[]{:S(2)}, u32[]{:S(2)}) %all-to-all-start) | async-done | bytes 524320 | tf_op jit(solution)/shard_map/all_to_all | solution.py:166
  88.5 1.5 %collective-permute-start.11 = (bf16[512,512]{1,0:T(8,128)(2,1)}, bf16[512,512]{1,0:T(8,128)(2,1)}, u32[]{:S(2)}, u32[]{:S(2)}) collective-permute-start(bf16[512,512]{1,0:T(8,128)(2,1)} %bitcast.13), channel_id=1, source_target_pairs={{0,1},{1,0},{2,3},{3,2},{4,5},{5,4},{6,7},{7,6},{8,9},{9,8},{10,11... | collective-permute-start | bytes 1572872 | tf_op jit(solution)/shard_map/ppermute | solution.py:227
  90.9 1.3 %collective-permute-start.8 = (bf16[128,1024]{1,0:T(8,128)(2,1)S(1)}, bf16[128,1024]{1,0:T(8,128)(2,1)}, u32[]{:S(2)}, u32[]{:S(2)}) collective-permute-start(bf16[128,1024]{1,0:T(8,128)(2,1)S(1)} %bitcast.30), channel_id=1, source_target_pairs={{4,0},{6,2},{5,1},{7,3},{12,8},{14,10},{13,9},{15,11},{20,16},{22,... | collective-permute-start | bytes 786440 | tf_op jit(solution)/shard_map/ppermute | solution.py:15
  94.2 1.9 %collective-permute-start.10 = (bf16[128,1024]{1,0:T(8,128)(2,1)}, bf16[128,1024]{1,0:T(8,128)(2,1)}, u32[]{:S(2)}, u32[]{:S(2)}) collective-permute-start(bf16[128,1024]{1,0:T(8,128)(2,1)} %collective-permute-done.9.refs_8_), channel_id=1, source_target_pairs={{2,0},{4,2},{6,4},{3,1},{5,3},{7,5},{10,8},{12,10},{14,12},{11,9},... | collective-permute-start | bytes 786440 | tf_op jit(solution)/shard_map/ppermute | solution.py:15
  96.1 3.0 %shard_map.112 = bf16[128,1024]{1,0:T(8,128)(2,1)} custom-call(f32[384,128]{1,0:T(8,128)S(1)} %and_convert_fusion.1.mask_ref, bf16[128,1024]{1,0:T(8,128)(2,1)S(1)} %bitcast.32, bf16[128,1024]{1,0:T(8,128)(2,1)S(1)} %fusion.9.after_ref.dctx_ref.refs_7_, bf16[128,1024]{1,0:T(8,128)(2,1)S(1)} %bitcast.35, f32[8,128]{1,0:T(8,128)S(1)} %shard_map.111.total_ref, ...), custom_call_target="tpu_custom_call" | custom-call | flops 301989888 | bytes 2822144 | tf_op jit(solution)/shard_map/pallas_call | solution.py:111
  99.1 3.8 %collective-permute-done.6 = f32[8,128]{1,0:T(8,128)S(1)} collective-permute-done((f32[8,128]{1,0:T(8,128)S(1)}, f32[8,128]{1,0:T(8,128)S(1)}, u32[]{:S(2)}, u32[]{:S(2)}) %collective-permute-start.6) | collective-permute-done | bytes 4128 | tf_op jit(solution)/shard_map/ppermute | solution.py:15
  102.9 5.2 %collective-permute-start.5 = (f32[8,128]{1,0:T(8,128)S(1)}, f32[8,128]{1,0:T(8,128)S(1)}, u32[]{:S(2)}, u32[]{:S(2)}) collective-permute-start(f32[8,128]{1,0:T(8,128)S(1)} %shard_map.111.total_ref), channel_id=1, source_target_pairs={{2,0},{4,2},{6,4},{3,1},{5,3},{7,5},{10,8},{12,10},{14,12},{11,9},... | collective-permute-start | bytes 12296 | tf_op jit(solution)/shard_map/ppermute | solution.py:15
  109.7 4.1 %shard_map.113 = (bf16[128,1024]{1,0:T(8,128)(2,1)}, bf16[128,1024]{1,0:T(8,128)(2,1)}) custom-call(f32[128,384]{1,0:T(8,128)S(1)} %and_convert_fusion.refs_0_, bf16[128,1024]{1,0:T(8,128)(2,1)S(1)} %bitcast.40, bf16[128,1024]{1,0:T(8,128)(2,1)S(1)} %bitcast.38, f32[8,384]{1,0:T(8,128)S(1)} %pad_maximum_fusion.1.refs_3_, bf16[128,1024]{1,0:T(8,128)(2,1)S(1)} %bitcast.33, ...), custom_call_target="tpu_custom_call" | custom-call | flops 402653184 | bytes 3616768 | tf_op jit(solution)/shard_map/pallas_call | solution.py:111
  116.2 3.3 %convolution_bitcast_fusion = f32[1,1024,1024]{2,1,0:T(8,128)} fusion(bf16[512,1024]{1,0:T(8,128)(2,1)S(1)} %constant_dynamic-update-slice_fusion, bf16[512,1024]{1,0:T(8,128)(2,1)S(1)} %copy-done.5), kind=kOutput, calls=%fused_computation.6 | convolution fusion | flops 1073741824 | bytes 6291456 | tf_op jit(solution)/shard_map/dot_general | solution.py:232
  (51 shorter events, 10.6 us)
Async XLA Ops:
  7.2 101.0 %all-gather.2.cloned.1.call-start = ((), (), s32[]{:S(2)}) async-start(), calls=%async_computation.1 | async-start | bytes 1310720 | tf_op jit(solution)/shard_map/all_gather | solution.py:142
  8.5 27.7 %copy-start.7 = (s32[4]{0:T(128)S(1)}, s32[4]{0:T(128)}, u32[]{:S(2)}) copy-start(s32[4]{0:T(128)} %param.15) | copy-start | bytes 52
  9.6 8.6 %collective-permute-start = (bf16[128,2048]{0,1:T(8,128)(2,1)S(1)}, bf16[128,2048]{0,1:T(8,128)(2,1)S(1)}, u32[]{:S(2)}, u32[]{:S(2)}) collective-permute-start(bf16[128,2048]{0,1:T(8,128)(2,1)S(1)} %bitcast.41), channel_id=1, source_target_pairs={{8,0},{16,8},{24,16},{9,1},{17,9},{25,17},{10,2},{18,10},{26,18},{... | collective-permute-start | bytes 1572872 | tf_op jit(solution)/shard_map/ppermute | solution.py:15
  19.2 13.9 %collective-permute-start.1 = (bf16[128,2048]{0,1:T(8,128)(2,1)}, bf16[128,2048]{0,1:T(8,128)(2,1)}, u32[]{:S(2)}, u32[]{:S(2)}) collective-permute-start(bf16[128,2048]{0,1:T(8,128)(2,1)} %fusion.12), channel_id=1, source_target_pairs={{16,0},{24,8},{17,1},{25,9},{18,2},{26,10},{19,3},{27,11},{20,4},{... | collective-permute-start | bytes 1572872 | tf_op jit(solution)/shard_map/ppermute | solution.py:15
  21.3 69.6 %collective-permute-start.3 = (bf16[128,2048]{1,0:T(8,128)(2,1)S(1)}, bf16[128,2048]{1,0:T(8,128)(2,1)S(1)}, u32[]{:S(2)}, u32[]{:S(2)}) collective-permute-start(bf16[128,2048]{1,0:T(8,128)(2,1)S(1)} %pad_maximum_fusion.refs_2_), channel_id=1, source_target_pairs={{0,4},{2,6},{1,5},{3,7},{8,12},{10,14},{9,13},{11,15},{16,20},{18,... | collective-permute-start | bytes 1572872 | tf_op jit(solution)/shard_map/ppermute | solution.py:15
  25.8 66.4 %collective-permute-start.4 = (bf16[128,2048]{1,0:T(8,128)(2,1)S(1)}, bf16[128,2048]{1,0:T(8,128)(2,1)S(1)}, u32[]{:S(2)}, u32[]{:S(2)}) collective-permute-start(bf16[128,2048]{1,0:T(8,128)(2,1)S(1)} %pad_maximum_fusion.refs_2_), channel_id=1, source_target_pairs={{0,2},{2,4},{4,6},{1,3},{3,5},{5,7},{8,10},{10,12},{12,14},{9,11},... | collective-permute-start | bytes 1572872 | tf_op jit(solution)/shard_map/ppermute | solution.py:15
  27.7 82.0 %collective-permute-start.7 = (bf16[128,1024]{1,0:T(8,128)(2,1)}, bf16[128,1024]{1,0:T(8,128)(2,1)S(1)}, u32[]{:S(2)}, u32[]{:S(2)}) collective-permute-start(bf16[128,1024]{1,0:T(8,128)(2,1)} %bitcast.29), channel_id=1, source_target_pairs={{2,0},{4,2},{6,4},{3,1},{5,3},{7,5},{10,8},{12,10},{14,12},{11,9},... | collective-permute-start | bytes 786440 | tf_op jit(solution)/shard_map/ppermute | solution.py:15
  34.6 14.1 %copy-start.4 = (bf16[128,2048]{0,1:T(8,128)(2,1)}, bf16[128,2048]{0,1:T(8,128)(2,1)S(1)}, u32[]{:S(2)}) copy-start(bf16[128,2048]{0,1:T(8,128)(2,1)S(1)} %get-tuple-element.17) | copy-start | bytes 1572868
  34.6 14.1 %collective-permute-start.2 = (bf16[128,2048]{0,1:T(8,128)(2,1)S(1)}, bf16[128,2048]{0,1:T(8,128)(2,1)S(1)}, u32[]{:S(2)}, u32[]{:S(2)}) collective-permute-start(bf16[128,2048]{0,1:T(8,128)(2,1)S(1)} %get-tuple-element.17), channel_id=1, source_target_pairs={{0,1},{1,0},{2,3},{3,2},{4,5},{5,4},{6,7},{7,6},{8,9},{9,8},{10,11... | collective-permute-start | bytes 1572872 | tf_op jit(solution)/shard_map/ppermute | solution.py:150
  36.4 21.0 %copy-start.6 = (s32[128]{0:T(128)}, s32[128]{0:T(128)S(1)}, u32[]{:S(2)}) copy-start(s32[128]{0:T(128)S(1)} %convert_reduce_fusion.2) | copy-start | bytes 1540
  49.9 38.7 %all-to-all-start = ((bf16[128,4,512]{2,0,1:T(8,128)(2,1)}), bf16[128,4,512]{2,0,1:T(8,128)(2,1)}, u32[]{:S(2)}, u32[]{:S(2)}) async-start(bf16[128,4,512]{2,0,1:T(8,128)(2,1)} %bitcast.11), calls=%async_computation | async-start | bytes 1048576 | tf_op jit(solution)/shard_map/all_to_all | solution.py:166
  54.2 36.6 %copy-start = (bf16[1,128,1024]{2,1,0:T(8,128)(2,1)S(1)}, bf16[1,128,1024]{2,1,0:T(8,128)(2,1)}, u32[]{:S(2)}) copy-start(bf16[1,128,1024]{2,1,0:T(8,128)(2,1)} %param.11) | copy-start | bytes 786436
  57.4 38.7 %copy-start.1 = (bf16[1,128,1024]{2,1,0:T(8,128)(2,1)S(1)}, bf16[1,128,1024]{2,1,0:T(8,128)(2,1)}, u32[]{:S(2)}) copy-start(bf16[1,128,1024]{2,1,0:T(8,128)(2,1)} %param.10) | copy-start | bytes 786436
  60.4 49.3 %copy-start.2 = (bf16[1,128,1024]{2,1,0:T(8,128)(2,1)S(1)}, bf16[1,128,1024]{2,1,0:T(8,128)(2,1)}, u32[]{:S(2)}) copy-start(bf16[1,128,1024]{2,1,0:T(8,128)(2,1)} %param.13) | copy-start | bytes 786436
  60.4 49.3 %copy-start.3 = (bf16[1,128,1024]{2,1,0:T(8,128)(2,1)S(1)}, bf16[1,128,1024]{2,1,0:T(8,128)(2,1)}, u32[]{:S(2)}) copy-start(bf16[1,128,1024]{2,1,0:T(8,128)(2,1)} %param.12) | copy-start | bytes 786436
  60.4 33.8 %collective-permute-start.9 = (bf16[128,1024]{1,0:T(8,128)(2,1)S(1)}, bf16[128,1024]{1,0:T(8,128)(2,1)}, u32[]{:S(2)}, u32[]{:S(2)}) collective-permute-start(bf16[128,1024]{1,0:T(8,128)(2,1)S(1)} %fusion.9.after_ref.dctx_ref.refs_7_), channel_id=1, source_target_pairs={{2,0},{4,2},{6,4},{3,1},{5,3},{7,5},{10,8},{12,10},{14,12},{11,9},... | collective-permute-start | bytes 786440 | tf_op jit(solution)/shard_map/ppermute | solution.py:15
  88.5 26.5 %collective-permute-start.11 = (bf16[512,512]{1,0:T(8,128)(2,1)}, bf16[512,512]{1,0:T(8,128)(2,1)}, u32[]{:S(2)}, u32[]{:S(2)}) collective-permute-start(bf16[512,512]{1,0:T(8,128)(2,1)} %bitcast.13), channel_id=1, source_target_pairs={{0,1},{1,0},{2,3},{3,2},{4,5},{5,4},{6,7},{7,6},{8,9},{9,8},{10,11... | collective-permute-start | bytes 1572872 | tf_op jit(solution)/shard_map/ppermute | solution.py:227
  90.9 18.8 %collective-permute-start.8 = (bf16[128,1024]{1,0:T(8,128)(2,1)S(1)}, bf16[128,1024]{1,0:T(8,128)(2,1)}, u32[]{:S(2)}, u32[]{:S(2)}) collective-permute-start(bf16[128,1024]{1,0:T(8,128)(2,1)S(1)} %bitcast.30), channel_id=1, source_target_pairs={{4,0},{6,2},{5,1},{7,3},{12,8},{14,10},{13,9},{15,11},{20,16},{22,... | collective-permute-start | bytes 786440 | tf_op jit(solution)/shard_map/ppermute | solution.py:15
  92.9 10.1 %collective-permute-start.6 = (f32[8,128]{1,0:T(8,128)S(1)}, f32[8,128]{1,0:T(8,128)S(1)}, u32[]{:S(2)}, u32[]{:S(2)}) collective-permute-start(f32[8,128]{1,0:T(8,128)S(1)} %shard_map.111.total_ref), channel_id=1, source_target_pairs={{4,0},{6,2},{5,1},{7,3},{12,8},{14,10},{13,9},{15,11},{20,16},{22,... | collective-permute-start | bytes 12296 | tf_op jit(solution)/shard_map/ppermute | solution.py:15
  94.2 15.5 %collective-permute-start.10 = (bf16[128,1024]{1,0:T(8,128)(2,1)}, bf16[128,1024]{1,0:T(8,128)(2,1)}, u32[]{:S(2)}, u32[]{:S(2)}) collective-permute-start(bf16[128,1024]{1,0:T(8,128)(2,1)} %collective-permute-done.9.refs_8_), channel_id=1, source_target_pairs={{2,0},{4,2},{6,4},{3,1},{5,3},{7,5},{10,8},{12,10},{14,12},{11,9},... | collective-permute-start | bytes 786440 | tf_op jit(solution)/shard_map/ppermute | solution.py:15
  102.9 6.7 %collective-permute-start.5 = (f32[8,128]{1,0:T(8,128)S(1)}, f32[8,128]{1,0:T(8,128)S(1)}, u32[]{:S(2)}, u32[]{:S(2)}) collective-permute-start(f32[8,128]{1,0:T(8,128)S(1)} %shard_map.111.total_ref), channel_id=1, source_target_pairs={{2,0},{4,2},{6,4},{3,1},{5,3},{7,5},{10,8},{12,10},{14,12},{11,9},... | collective-permute-start | bytes 12296 | tf_op jit(solution)/shard_map/ppermute | solution.py:15
  108.1 8.0 %copy-start.5 = (bf16[512,1024]{1,0:T(8,128)(2,1)S(1)}, bf16[512,1024]{1,0:T(8,128)(2,1)}, u32[]{:S(2)}) copy-start(bf16[512,1024]{1,0:T(8,128)(2,1)} %all-gather.2.cloned.1.call-done) | copy-start | bytes 3145732
Sparse Core Ops, SparseCore 0:
  31.8 43.5 all-gather.1

commit v5 on v4

--- a/solution.py
+++ b/solution.py
@@ -50,8 +50,8 @@
     return jnp.sum(jnp.transpose(product), axis=0, keepdims=True)
 
 
-def totals_kernel(after_ref, mask_ref, query_ref, *refs):
-    del after_ref
+def totals_kernel(ahead, *refs):
+    mask_ref, query_ref, *refs = refs[ahead:]
     kv_refs, total_ref = refs[:-1], refs[-1]
     allowed = mask_ref[...] > 0.0
     for head in range(query_ref.shape[1] // HD):
@@ -179,9 +179,9 @@
     work = 2 * window * rows * width
     kv_win = kv_sets[::-1]
     (total,) = local_kernel(
-        totals_kernel,
+        lambda *refs: totals_kernel(REACH + 1, *refs),
         [jax.ShapeDtypeStruct((head_count, rows), jnp.float32)],
-        (d_context, allowed, queries[0], *kv_win),
+        (d_context, *query_sets[1:], allowed, queries[0], *kv_win),
         work,
     )
     total_sets = [total]

time: 129 us -> 128 us (level); the launches traced: 126 us -> 127 us
    ppermute x10, starting transfers between devices: 26.1 us -> 23 us  [passed_along(): lax.ppermute(value, axis, [(source, source + steps) for source in range(l...]
    all_to_all x1, starting transfers between devices: 4.13 us -> 6.46 us  [on_device(): lax.all_to_all(grad_share.reshape(rows, n_dp * share), 'dp', split_axis=1...]
    unnamed x18 -> x16, local copies, waits for them, and re-layouts: 2.66 us -> 2.66 us
  transfers between devices with their start and end apart: 14 -> 14, of which waited for: 5 -> 4; matrix products, arithmetic and copies ran while one was open for 11% -> 11% of each run, Pallas kernels for 6% -> 7%
where the time goes in v5:
time: 128 us; the launch traced here: 127 us
  waiting for transfers between devices  49.3 us (39%)
  starting transfers between devices  32.5 us (25%)
  between operations  14.4 us (11%)
  matrix products  9.43 us (7%)
  Pallas kernels  8.69 us (7%)
  local copies, waits for them, and re-layouts  7.44 us (6%)
  other arithmetic  5.21 us (4%)
    all_to_all x1, waiting for transfers between devices, on_device(): lax.all_to_all(grad_share.reshape(rows, n_dp * share), 'dp', split_axis=1...  26.2 us
    ppermute x10, starting transfers between devices, passed_along(): lax.ppermute(value, axis, [(source, source + steps) for source in range(l...  23 us
    ppermute x1, waiting for transfers between devices, on_device(): lax.ppermute(grad_local, 'tensor', [(i, (i + step) % n_tensor) for i in r...  12.2 us
    ppermute x10, waiting for transfers between devices, passed_along(): lax.ppermute(value, axis, [(source, source + steps) for source in range(l...  11 us
    pallas_call x3, Pallas kernels, local_kernel(): pl.pallas_call(body, out_shape=shapes, in_specs=[whole] * len(operands),...  8.69 us
    all_to_all x1, starting transfers between devices, on_device(): lax.all_to_all(grad_share.reshape(rows, n_dp * share), 'dp', split_axis=1...  6.46 us
    dot_general x2, matrix products, on_device(): jnp.dot(part, weight, preferred_element_type=jnp.float32)  6.12 us
    dot_general x1, matrix products, on_device(): lax.dot_general(grad_blocks, context_all, (((0,), (0,)), ((), ())), prefe...  3.31 us
  transfers between devices with their start and end apart: 14, of which 4 were waited for; matrix products, arithmetic and copies ran while one was open for 11% of the time, Pallas kernels for 7%

profile of v5, /device:TPU:12, one launch (start us, length us, event | category | flops | bytes accessed | tf_op | source)
XLA Modules:
  0.0 127.1 jit_solution(1512829887667605004)
XLA Ops:
  7.2 1.3 %copy.16 = bf16[1,128,2048]{1,2,0:T(8,128)(2,1)S(1)} copy(bf16[1,128,2048]{2,1,0:T(8,128)(2,1)} %param.9) | data formatting | bytes 1048576 | tf_op args[1]
  9.6 1.9 %collective-permute-start = (bf16[128,2048]{0,1:T(8,128)(2,1)S(1)}, bf16[128,2048]{0,1:T(8,128)(2,1)S(1)}, u32[]{:S(2)}, u32[]{:S(2)}) collective-permute-start(bf16[128,2048]{0,1:T(8,128)(2,1)S(1)} %bitcast.41), channel_id=1, source_target_pairs={{8,0},{16,8},{24,16},{9,1},{17,9},{25,17},{10,2},{18,10},{26,18},{... | collective-permute-start | bytes 1572872 | tf_op jit(solution)/shard_map/ppermute | solution.py:15
  11.5 6.7 %collective-permute-done = bf16[128,2048]{0,1:T(8,128)(2,1)S(1)} collective-permute-done((bf16[128,2048]{0,1:T(8,128)(2,1)S(1)}, bf16[128,2048]{0,1:T(8,128)(2,1)S(1)}, u32[]{:S(2)}, u32[]{:S(2)}) %collective-permute-start) | collective-permute-done | bytes 524320 | tf_op jit(solution)/shard_map/ppermute | solution.py:15
  19.2 2.1 %collective-permute-start.1 = (bf16[128,2048]{0,1:T(8,128)(2,1)}, bf16[128,2048]{0,1:T(8,128)(2,1)}, u32[]{:S(2)}, u32[]{:S(2)}) collective-permute-start(bf16[128,2048]{0,1:T(8,128)(2,1)} %fusion.12), channel_id=1, source_target_pairs={{16,0},{24,8},{17,1},{25,9},{18,2},{26,10},{19,3},{27,11},{20,4},{... | collective-permute-start | bytes 1572872 | tf_op jit(solution)/shard_map/ppermute | solution.py:15
  21.3 2.3 %collective-permute-start.3 = (bf16[128,1024]{1,0:T(8,128)(2,1)}, bf16[128,1024]{1,0:T(8,128)(2,1)S(1)}, u32[]{:S(2)}, u32[]{:S(2)}) collective-permute-start(bf16[128,1024]{1,0:T(8,128)(2,1)} %bitcast.32), channel_id=1, source_target_pairs={{2,0},{4,2},{6,4},{3,1},{5,3},{7,5},{10,8},{12,10},{14,12},{11,9},... | collective-permute-start | bytes 786440 | tf_op jit(solution)/shard_map/ppermute | solution.py:15
  24.9 6.2 %collective-permute-start.5 = (bf16[128,2048]{1,0:T(8,128)(2,1)S(1)}, bf16[128,2048]{1,0:T(8,128)(2,1)S(1)}, u32[]{:S(2)}, u32[]{:S(2)}) collective-permute-start(bf16[128,2048]{1,0:T(8,128)(2,1)S(1)} %pad_maximum_fusion.refs_7_.refs_2_), channel_id=1, source_target_pairs={{0,4},{2,6},{1,5},{3,7},{8,12},{10,14},{9,13},{11,15},{16,20},{18,... | collective-permute-start | bytes 1572872 | tf_op jit(solution)/shard_map/ppermute | solution.py:15
  31.1 1.9 %collective-permute-start.6 = (bf16[128,2048]{1,0:T(8,128)(2,1)S(1)}, bf16[128,2048]{1,0:T(8,128)(2,1)S(1)}, u32[]{:S(2)}, u32[]{:S(2)}) collective-permute-start(bf16[128,2048]{1,0:T(8,128)(2,1)S(1)} %pad_maximum_fusion.refs_7_.refs_2_), channel_id=1, source_target_pairs={{0,2},{2,4},{4,6},{1,3},{3,5},{5,7},{8,10},{10,12},{12,14},{9,11},... | collective-permute-start | bytes 1572872 | tf_op jit(solution)/shard_map/ppermute | solution.py:15
  33.1 1.3 %copy.15 = bf16[128,2048]{0,1:T(8,128)(2,1)S(1)} copy(bf16[128,2048]{1,0:T(8,128)(2,1)} %param.8) | data formatting | bytes 1048576 | tf_op args[0]
  34.6 1.4 %constant_dynamic-update-slice_fusion.3 = (bf16[128,4096]{0,1:T(8,128)(2,1)S(1)}, bf16[128,2048]{0,1:T(8,128)(2,1)S(1)}) fusion(bf16[128,4096]{0,1:T(8,128)(2,1)S(1)} %broadcast_in_dim.30, s32[]{:T(128)S(6)} %select_n.29, bf16[128,2048]{0,1:T(8,128)(2,1)} %collective-permute-done.1, bf16[128,2048]{0,1:T(8,128)(2,1)S(1)} %collective-permute-done, ...), kind=kLoop, calls=%fused_computation.22 | loop fusion | flops 2359296 | bytes 3145732 | tf_op jit(solution)/shard_map/dynamic_update_slice | solution.py:154
  36.0 1.6 %collective-permute-start.2 = (bf16[128,2048]{0,1:T(8,128)(2,1)S(1)}, bf16[128,2048]{0,1:T(8,128)(2,1)S(1)}, u32[]{:S(2)}, u32[]{:S(2)}) collective-permute-start(bf16[128,2048]{0,1:T(8,128)(2,1)S(1)} %get-tuple-element.17), channel_id=1, source_target_pairs={{0,1},{1,0},{2,3},{3,2},{4,5},{5,4},{6,7},{7,6},{8,9},{9,8},{10,11... | collective-permute-start | bytes 1572872 | tf_op jit(solution)/shard_map/ppermute | solution.py:150
  37.9 12.2 %collective-permute-done.2 = bf16[128,2048]{0,1:T(8,128)(2,1)S(1)} collective-permute-done((bf16[128,2048]{0,1:T(8,128)(2,1)S(1)}, bf16[128,2048]{0,1:T(8,128)(2,1)S(1)}, u32[]{:S(2)}, u32[]{:S(2)}) %collective-permute-start.2) | collective-permute-done | bytes 524320 | tf_op jit(solution)/shard_map/ppermute | solution.py:150
  51.2 6.5 %all-to-all-start = ((bf16[128,4,512]{2,0,1:T(8,128)(2,1)}), bf16[128,4,512]{2,0,1:T(8,128)(2,1)}, u32[]{:S(2)}, u32[]{:S(2)}) async-start(bf16[128,4,512]{2,0,1:T(8,128)(2,1)} %bitcast.11), calls=%async_computation | async-start | bytes 1048576 | tf_op jit(solution)/shard_map/all_to_all | solution.py:166
  57.9 3.1 %fusion.2 = f32[128,1024]{1,0:T(8,128)S(1)} fusion(bf16[128,2048]{0,1:T(8,128)(2,1)} %copy-done.4, bf16[1,4096,1024]{2,1,0:T(8,128)(2,1)} %param.14, s32[]{:T(128)S(6)} %select_n.29), kind=kOutput, calls=%fused_computation.2 | convolution fusion | flops 536870912 | bytes 5242884 | tf_op jit(solution)/shard_map/dot_general | solution.py:156
  61.1 3.0 %fusion.9.refs_0_.dctx_ref.refs_7_ = bf16[128,1024]{1,0:T(8,128)(2,1)S(1)} fusion(f32[128,1024]{1,0:T(8,128)S(1)} %fusion.2, bf16[128,2048]{0,1:T(8,128)(2,1)S(1)} %collective-permute-done.2, bf16[1,4096,1024]{2,1,0:T(8,128)(2,1)} %param.14, s32[]{:T(128)S(6)} %select_n.30), kind=kOutput, calls=%fused_computation.8 | convolution fusion | flops 537133056 | bytes 5505028 | tf_op jit(solution)/shard_map/dot_general | solution.py:156
  64.1 2.1 %collective-permute-start.9 = (bf16[128,1024]{1,0:T(8,128)(2,1)S(1)}, bf16[128,1024]{1,0:T(8,128)(2,1)}, u32[]{:S(2)}, u32[]{:S(2)}) collective-permute-start(bf16[128,1024]{1,0:T(8,128)(2,1)S(1)} %fusion.9.refs_0_.dctx_ref.refs_7_), channel_id=1, source_target_pairs={{2,0},{4,2},{6,4},{3,1},{5,3},{7,5},{10,8},{12,10},{14,12},{11,9},... | collective-permute-start | bytes 786440 | tf_op jit(solution)/shard_map/ppermute | solution.py:15
  66.7 26.2 %all-to-all-done = bf16[128,4,512]{2,0,1:T(8,128)(2,1)} async-done(((bf16[128,4,512]{2,0,1:T(8,128)(2,1)}), bf16[128,4,512]{2,0,1:T(8,128)(2,1)}, u32[]{:S(2)}, u32[]{:S(2)}) %all-to-all-start) | async-done | bytes 524320 | tf_op jit(solution)/shard_map/all_to_all | solution.py:166
  92.9 1.5 %collective-permute-start.11 = (bf16[512,512]{1,0:T(8,128)(2,1)}, bf16[512,512]{1,0:T(8,128)(2,1)}, u32[]{:S(2)}, u32[]{:S(2)}) collective-permute-start(bf16[512,512]{1,0:T(8,128)(2,1)} %bitcast.13), channel_id=1, source_target_pairs={{0,1},{1,0},{2,3},{3,2},{4,5},{5,4},{6,7},{7,6},{8,9},{9,8},{10,11... | collective-permute-start | bytes 1572872 | tf_op jit(solution)/shard_map/ppermute | solution.py:227
  95.2 1.6 %shard_map.111.total_ref = f32[8,128]{1,0:T(8,128)S(1)} custom-call(bf16[128,1024]{1,0:T(8,128)(2,1)S(1)} %fusion.9.refs_0_.dctx_ref.refs_7_, bf16[128,1024]{1,0:T(8,128)(2,1)S(1)} %collective-permute-done.3.refs_1_.refs_5_, bf16[128,1024]{1,0:T(8,128)(2,1)} %collective-permute-done.4.refs_2_.refs_6_, f32[384,128]{1,0:T(8,128)S(1)} %and_convert_fusion.1.refs_3_.mask_ref, ...), custom_call_target="tpu_custom_call" | custom-call | flops 100663296 | bytes 2822144 | tf_op jit(solution)/shard_map/pallas_call | solution.py:111
  98.1 1.9 %collective-permute-start.7 = (f32[8,128]{1,0:T(8,128)S(1)}, f32[8,128]{1,0:T(8,128)S(1)}, u32[]{:S(2)}, u32[]{:S(2)}) collective-permute-start(f32[8,128]{1,0:T(8,128)S(1)} %shard_map.111.total_ref), channel_id=1, source_target_pairs={{2,0},{4,2},{6,4},{3,1},{5,3},{7,5},{10,8},{12,10},{14,12},{11,9},... | collective-permute-start | bytes 12296 | tf_op jit(solution)/shard_map/ppermute | solution.py:15
  100.1 1.9 %collective-permute-start.10 = (bf16[128,1024]{1,0:T(8,128)(2,1)}, bf16[128,1024]{1,0:T(8,128)(2,1)}, u32[]{:S(2)}, u32[]{:S(2)}) collective-permute-start(bf16[128,1024]{1,0:T(8,128)(2,1)} %collective-permute-done.9.refs_8_), channel_id=1, source_target_pairs={{2,0},{4,2},{6,4},{3,1},{5,3},{7,5},{10,8},{12,10},{14,12},{11,9},... | collective-permute-start | bytes 786440 | tf_op jit(solution)/shard_map/ppermute | solution.py:15
  102.0 3.0 %shard_map.112 = bf16[128,1024]{1,0:T(8,128)(2,1)} custom-call(f32[384,128]{1,0:T(8,128)S(1)} %and_convert_fusion.1.refs_3_.mask_ref, bf16[128,1024]{1,0:T(8,128)(2,1)S(1)} %bitcast.35, bf16[128,1024]{1,0:T(8,128)(2,1)S(1)} %fusion.9.refs_0_.dctx_ref.refs_7_, bf16[128,1024]{1,0:T(8,128)(2,1)S(1)} %bitcast.30, f32[8,128]{1,0:T(8,128)S(1)} %shard_map.111.total_ref, ...), custom_call_target="tpu_custom_call" | custom-call | flops 301989888 | bytes 2822144 | tf_op jit(solution)/shard_map/pallas_call | solution.py:111
  106.2 4.3 %collective-permute-done.10.refs_9_ = bf16[128,1024]{1,0:T(8,128)(2,1)} collective-permute-done((bf16[128,1024]{1,0:T(8,128)(2,1)}, bf16[128,1024]{1,0:T(8,128)(2,1)}, u32[]{:S(2)}, u32[]{:S(2)}) %collective-permute-start.10) | collective-permute-done | bytes 262176 | tf_op jit(solution)/shard_map/ppermute | solution.py:15
  110.5 4.1 %shard_map.113 = (bf16[128,1024]{1,0:T(8,128)(2,1)}, bf16[128,1024]{1,0:T(8,128)(2,1)}) custom-call(f32[128,384]{1,0:T(8,128)S(1)} %and_convert_fusion.refs_0_, bf16[128,1024]{1,0:T(8,128)(2,1)S(1)} %bitcast.40, bf16[128,1024]{1,0:T(8,128)(2,1)S(1)} %bitcast.38, f32[8,384]{1,0:T(8,128)S(1)} %pad_maximum_fusion.1.refs_3_, bf16[128,1024]{1,0:T(8,128)(2,1)S(1)} %bitcast.36, ...), custom_call_target="tpu_custom_call" | custom-call | flops 402653184 | bytes 3616768 | tf_op jit(solution)/shard_map/pallas_call | solution.py:111
  116.9 3.3 %convolution_bitcast_fusion = f32[1,1024,1024]{2,1,0:T(8,128)} fusion(bf16[512,1024]{1,0:T(8,128)(2,1)S(1)} %constant_dynamic-update-slice_fusion, bf16[512,1024]{1,0:T(8,128)(2,1)S(1)} %copy-done.5), kind=kOutput, calls=%fused_computation.6 | convolution fusion | flops 1073741824 | bytes 6291456 | tf_op jit(solution)/shard_map/dot_general | solution.py:232
  (49 shorter events, 11.3 us)
Async XLA Ops:
  7.2 97.8 %all-gather.2.cloned.1.call-start = ((), (), s32[]{:S(2)}) async-start(), calls=%async_computation.1 | async-start | bytes 1310720 | tf_op jit(solution)/shard_map/all_gather | solution.py:142
  8.5 29.0 %copy-start.6 = (s32[4]{0:T(128)S(1)}, s32[4]{0:T(128)}, u32[]{:S(2)}) copy-start(s32[4]{0:T(128)} %param.15) | copy-start | bytes 52
  9.6 8.6 %collective-permute-start = (bf16[128,2048]{0,1:T(8,128)(2,1)S(1)}, bf16[128,2048]{0,1:T(8,128)(2,1)S(1)}, u32[]{:S(2)}, u32[]{:S(2)}) collective-permute-start(bf16[128,2048]{0,1:T(8,128)(2,1)S(1)} %bitcast.41), channel_id=1, source_target_pairs={{8,0},{16,8},{24,16},{9,1},{17,9},{25,17},{10,2},{18,10},{26,18},{... | collective-permute-start | bytes 1572872 | tf_op jit(solution)/shard_map/ppermute | solution.py:15
  19.2 15.3 %collective-permute-start.1 = (bf16[128,2048]{0,1:T(8,128)(2,1)}, bf16[128,2048]{0,1:T(8,128)(2,1)}, u32[]{:S(2)}, u32[]{:S(2)}) collective-permute-start(bf16[128,2048]{0,1:T(8,128)(2,1)} %fusion.12), channel_id=1, source_target_pairs={{16,0},{24,8},{17,1},{25,9},{18,2},{26,10},{19,3},{27,11},{20,4},{... | collective-permute-start | bytes 1572872 | tf_op jit(solution)/shard_map/ppermute | solution.py:15
  21.3 45.5 %collective-permute-start.3 = (bf16[128,1024]{1,0:T(8,128)(2,1)}, bf16[128,1024]{1,0:T(8,128)(2,1)S(1)}, u32[]{:S(2)}, u32[]{:S(2)}) collective-permute-start(bf16[128,1024]{1,0:T(8,128)(2,1)} %bitcast.32), channel_id=1, source_target_pairs={{2,0},{4,2},{6,4},{3,1},{5,3},{7,5},{10,8},{12,10},{14,12},{11,9},... | collective-permute-start | bytes 786440 | tf_op jit(solution)/shard_map/ppermute | solution.py:15
  23.6 71.5 %collective-permute-start.4 = (bf16[128,1024]{1,0:T(8,128)(2,1)}, bf16[128,1024]{1,0:T(8,128)(2,1)}, u32[]{:S(2)}, u32[]{:S(2)}) collective-permute-start(bf16[128,1024]{1,0:T(8,128)(2,1)} %bitcast.33), channel_id=1, source_target_pairs={{4,0},{6,2},{5,1},{7,3},{12,8},{14,10},{13,9},{15,11},{20,16},{22,... | collective-permute-start | bytes 786440 | tf_op jit(solution)/shard_map/ppermute | solution.py:15
  24.9 70.3 %collective-permute-start.5 = (bf16[128,2048]{1,0:T(8,128)(2,1)S(1)}, bf16[128,2048]{1,0:T(8,128)(2,1)S(1)}, u32[]{:S(2)}, u32[]{:S(2)}) collective-permute-start(bf16[128,2048]{1,0:T(8,128)(2,1)S(1)} %pad_maximum_fusion.refs_7_.refs_2_), channel_id=1, source_target_pairs={{0,4},{2,6},{1,5},{3,7},{8,12},{10,14},{9,13},{11,15},{16,20},{18,... | collective-permute-start | bytes 1572872 | tf_op jit(solution)/shard_map/ppermute | solution.py:15
  31.1 64.1 %collective-permute-start.6 = (bf16[128,2048]{1,0:T(8,128)(2,1)S(1)}, bf16[128,2048]{1,0:T(8,128)(2,1)S(1)}, u32[]{:S(2)}, u32[]{:S(2)}) collective-permute-start(bf16[128,2048]{1,0:T(8,128)(2,1)S(1)} %pad_maximum_fusion.refs_7_.refs_2_), channel_id=1, source_target_pairs={{0,2},{2,4},{4,6},{1,3},{3,5},{5,7},{8,10},{10,12},{12,14},{9,11},... | collective-permute-start | bytes 1572872 | tf_op jit(solution)/shard_map/ppermute | solution.py:15
  36.0 14.1 %copy-start.4 = (bf16[128,2048]{0,1:T(8,128)(2,1)}, bf16[128,2048]{0,1:T(8,128)(2,1)S(1)}, u32[]{:S(2)}) copy-start(bf16[128,2048]{0,1:T(8,128)(2,1)S(1)} %get-tuple-element.17) | copy-start | bytes 1572868
  36.0 14.1 %collective-permute-start.2 = (bf16[128,2048]{0,1:T(8,128)(2,1)S(1)}, bf16[128,2048]{0,1:T(8,128)(2,1)S(1)}, u32[]{:S(2)}, u32[]{:S(2)}) collective-permute-start(bf16[128,2048]{0,1:T(8,128)(2,1)S(1)} %get-tuple-element.17), channel_id=1, source_target_pairs={{0,1},{1,0},{2,3},{3,2},{4,5},{5,4},{6,7},{7,6},{8,9},{9,8},{10,11... | collective-permute-start | bytes 1572872 | tf_op jit(solution)/shard_map/ppermute | solution.py:150
  51.2 41.6 %all-to-all-start = ((bf16[128,4,512]{2,0,1:T(8,128)(2,1)}), bf16[128,4,512]{2,0,1:T(8,128)(2,1)}, u32[]{:S(2)}, u32[]{:S(2)}) async-start(bf16[128,4,512]{2,0,1:T(8,128)(2,1)} %bitcast.11), calls=%async_computation | async-start | bytes 1048576 | tf_op jit(solution)/shard_map/all_to_all | solution.py:166
  57.9 37.3 %copy-start.1 = (bf16[1,128,1024]{2,1,0:T(8,128)(2,1)S(1)}, bf16[1,128,1024]{2,1,0:T(8,128)(2,1)}, u32[]{:S(2)}) copy-start(bf16[1,128,1024]{2,1,0:T(8,128)(2,1)} %param.11) | copy-start | bytes 786436
  61.1 40.9 %copy-start = (bf16[1,128,1024]{2,1,0:T(8,128)(2,1)S(1)}, bf16[1,128,1024]{2,1,0:T(8,128)(2,1)}, u32[]{:S(2)}) copy-start(bf16[1,128,1024]{2,1,0:T(8,128)(2,1)} %param.10) | copy-start | bytes 786436
  64.1 46.4 %copy-start.2 = (bf16[1,128,1024]{2,1,0:T(8,128)(2,1)S(1)}, bf16[1,128,1024]{2,1,0:T(8,128)(2,1)}, u32[]{:S(2)}) copy-start(bf16[1,128,1024]{2,1,0:T(8,128)(2,1)} %param.13) | copy-start | bytes 786436
  64.1 46.4 %copy-start.3 = (bf16[1,128,1024]{2,1,0:T(8,128)(2,1)S(1)}, bf16[1,128,1024]{2,1,0:T(8,128)(2,1)}, u32[]{:S(2)}) copy-start(bf16[1,128,1024]{2,1,0:T(8,128)(2,1)} %param.12) | copy-start | bytes 786436
  64.1 36.0 %collective-permute-start.9 = (bf16[128,1024]{1,0:T(8,128)(2,1)S(1)}, bf16[128,1024]{1,0:T(8,128)(2,1)}, u32[]{:S(2)}, u32[]{:S(2)}) collective-permute-start(bf16[128,1024]{1,0:T(8,128)(2,1)S(1)} %fusion.9.refs_0_.dctx_ref.refs_7_), channel_id=1, source_target_pairs={{2,0},{4,2},{6,4},{3,1},{5,3},{7,5},{10,8},{12,10},{14,12},{11,9},... | collective-permute-start | bytes 786440 | tf_op jit(solution)/shard_map/ppermute | solution.py:15
  92.9 22.9 %collective-permute-start.11 = (bf16[512,512]{1,0:T(8,128)(2,1)}, bf16[512,512]{1,0:T(8,128)(2,1)}, u32[]{:S(2)}, u32[]{:S(2)}) collective-permute-start(bf16[512,512]{1,0:T(8,128)(2,1)} %bitcast.13), channel_id=1, source_target_pairs={{0,1},{1,0},{2,3},{3,2},{4,5},{5,4},{6,7},{7,6},{8,9},{9,8},{10,11... | collective-permute-start | bytes 1572872 | tf_op jit(solution)/shard_map/ppermute | solution.py:227
  96.8 9.3 %collective-permute-start.8 = (f32[8,128]{1,0:T(8,128)S(1)}, f32[8,128]{1,0:T(8,128)S(1)}, u32[]{:S(2)}, u32[]{:S(2)}) collective-permute-start(f32[8,128]{1,0:T(8,128)S(1)} %shard_map.111.total_ref), channel_id=1, source_target_pairs={{4,0},{6,2},{5,1},{7,3},{12,8},{14,10},{13,9},{15,11},{20,16},{22,... | collective-permute-start | bytes 12296 | tf_op jit(solution)/shard_map/ppermute | solution.py:15
  98.1 8.0 %collective-permute-start.7 = (f32[8,128]{1,0:T(8,128)S(1)}, f32[8,128]{1,0:T(8,128)S(1)}, u32[]{:S(2)}, u32[]{:S(2)}) collective-permute-start(f32[8,128]{1,0:T(8,128)S(1)} %shard_map.111.total_ref), channel_id=1, source_target_pairs={{2,0},{4,2},{6,4},{3,1},{5,3},{7,5},{10,8},{12,10},{14,12},{11,9},... | collective-permute-start | bytes 12296 | tf_op jit(solution)/shard_map/ppermute | solution.py:15
  100.1 10.4 %collective-permute-start.10 = (bf16[128,1024]{1,0:T(8,128)(2,1)}, bf16[128,1024]{1,0:T(8,128)(2,1)}, u32[]{:S(2)}, u32[]{:S(2)}) collective-permute-start(bf16[128,1024]{1,0:T(8,128)(2,1)} %collective-permute-done.9.refs_8_), channel_id=1, source_target_pairs={{2,0},{4,2},{6,4},{3,1},{5,3},{7,5},{10,8},{12,10},{14,12},{11,9},... | collective-permute-start | bytes 786440 | tf_op jit(solution)/shard_map/ppermute | solution.py:15
  105.0 11.9 %copy-start.5 = (bf16[512,1024]{1,0:T(8,128)(2,1)S(1)}, bf16[512,1024]{1,0:T(8,128)(2,1)}, u32[]{:S(2)}) copy-start(bf16[512,1024]{1,0:T(8,128)(2,1)} %all-gather.2.cloned.1.call-done) | copy-start | bytes 3145732
Sparse Core Ops, SparseCore 0:
  33.2 47.7 all-gather.1
